TPU v7x, 128 devices: a whole 4x4x4 slice. The times are simulated.
128 devices in a mesh: row: 4 (over y_hi, core), col: 32 (over z, y_lo, x).
Axes of the slice: x: 4, y: 4 (y_hi: 2, y_lo: 2; y = y_hi * 2 + y_lo), z: 4, core: 2. Of those that a mesh axis runs over, the one named last changes fastest.
Arguments:
- activations: bfloat16 [4096, 8192], P('row', 'col'), may hold values from -90 to 90
- norm_gain: bfloat16 [8192], P('col'), may hold values from 0.099609375 to 1.8984375
- w_query: bfloat16 [8192, 8192], P('row', 'col'), may hold values from -0.26516504 to 0.26516504
- w_key: bfloat16 [8192, 1024], P('row'), may hold values from -0.044194174 to 0.044194174
- w_value: bfloat16 [8192, 1024], P('row'), may hold values from -0.0625 to 0.0625
- w_out: bfloat16 [8192, 8192], P('row', 'col'), may hold values from -0.0625 to 0.0625
Outputs:
- output: bfloat16 [4096, 8192], P('row', 'col')
All inputs are finite; a program needn't handle non-finite values.
Results may differ from a plain program's by a relative error of at most 0.018.
Values may be sent and summed in bfloat16 or wider, within the bound.
A program may use at most 128 MiB of HBM per device.

v0:
```python
import jax
import jax.numpy as jnp
from jax import lax
from jax.sharding import PartitionSpec as P

HEADS = 64
KV_HEADS = 8
HEAD_DIM = 128


def rope_tables(count, offset, head_size):
    half_size = head_size // 2
    exponent = jnp.arange(half_size, dtype=jnp.float32) * (2.0 / head_size)
    frequency = jnp.exp(-jnp.log(500000.0) * exponent)
    position = (offset + jnp.arange(count, dtype=jnp.int32)).astype(jnp.float32)
    angles = position[:, None] * frequency[None, :]
    return (jnp.cos(angles), jnp.sin(angles))


def rotate(stacked, cos_table, sin_table):
    half_size = stacked.shape[-1] // 2
    leading = stacked[..., :half_size]
    trailing = stacked[..., half_size:]
    cosine = cos_table[:, None, :]
    sine_part = sin_table[:, None, :]
    return jnp.concatenate(
        [leading * cosine - trailing * sine_part, trailing * cosine + leading * sine_part], axis=-1
    )


def local(activations, norm_gain, w_query, w_key, w_value, w_out):
    tok_rows = activations.shape[0]
    row_index = lax.axis_index("row")
    col_index = lax.axis_index("col")
    head_size = HEAD_DIM
    q_width = w_query.shape[1]
    heads_local = q_width // head_size
    group_size = HEADS // KV_HEADS
    kv_count = max(1, heads_local // group_size)
    repeats = heads_local // kv_count
    model_width = activations.shape[1] * lax.axis_size("col")
    kv_first = col_index * heads_local // group_size
    key_cols = lax.dynamic_slice_in_dim(w_key, kv_first * head_size, kv_count * head_size, 1)
    value_cols = lax.dynamic_slice_in_dim(w_value, kv_first * head_size, kv_count * head_size, 1)
    local_wide = activations.astype(jnp.float32)
    square_total = lax.psum(jnp.sum(local_wide * local_wide, axis=1), "col")
    inverse_rms = lax.rsqrt(square_total / model_width + 1e-05)
    normed = (local_wide * inverse_rms[:, None] * norm_gain.astype(jnp.float32)[None, :]).astype(
        jnp.bfloat16
    )
    hidden = lax.all_gather(normed, "col", axis=1, tiled=True)

    def contract(piece):
        return jnp.dot(hidden, piece, preferred_element_type=jnp.float32)

    query = contract(lax.all_gather(w_query, "row", axis=0, tiled=True))
    pieces = (
        lax.all_gather(key_cols, "row", axis=0, tiled=True),
        lax.all_gather(value_cols, "row", axis=0, tiled=True),
    )
    key_part = contract(pieces[0])
    value_part = contract(pieces[1])
    key_mine = key_part.astype(jnp.bfloat16)
    value_mine = value_part.astype(jnp.bfloat16)
    offset = row_index * tok_rows
    cos_table, sin_table = rope_tables(tok_rows, offset, head_size)
    query_rot = rotate(
        query.reshape(tok_rows, heads_local, head_size), cos_table, sin_table
    ).astype(jnp.bfloat16)
    key_rot = rotate(
        key_mine.astype(jnp.float32).reshape(tok_rows, kv_count, head_size), cos_table, sin_table
    ).astype(jnp.bfloat16)
    value_heads = value_mine.reshape(tok_rows, kv_count, head_size)
    query_pos = offset + jnp.arange(tok_rows, dtype=jnp.int32)
    score_scale = head_size ** (-0.5)
    pieces = (
        lax.all_gather(key_rot, "row", axis=0, tiled=True),
        lax.all_gather(value_heads, "row", axis=0, tiled=True),
    )
    running_max = jnp.full((tok_rows, heads_local), -1e30, jnp.float32)
    key_piece = jnp.repeat(pieces[0], repeats, axis=1)
    value_piece = jnp.repeat(pieces[1], repeats, axis=1)
    scores = (
        jnp.einsum("qhd,khd->qhk", query_rot, key_piece, preferred_element_type=jnp.float32)
        * score_scale
    )
    key_pos = jnp.arange(key_piece.shape[0], dtype=jnp.int32)
    allowed = (key_pos[None, :] <= query_pos[:, None])[:, None, :]
    masked = jnp.where(allowed, scores, -1e30)
    new_max = jnp.maximum(running_max, jnp.max(masked, axis=2))
    exponentials = jnp.where(allowed, jnp.exp(masked - new_max[:, :, None]), 0.0)
    new_sum = jnp.sum(exponentials, axis=2)
    mixed = jnp.einsum(
        "qhk,khd->qhd",
        exponentials.astype(jnp.bfloat16),
        value_piece,
        preferred_element_type=jnp.float32,
    )
    attended = (mixed / new_sum[:, :, None]).astype(jnp.bfloat16).reshape(tok_rows, q_width)
    all_heads = lax.all_gather(attended, "col", axis=1, tiled=True)
    result = jnp.dot(
        all_heads,
        lax.all_gather(w_out, "row", axis=0, tiled=True),
        preferred_element_type=jnp.float32,
    )
    return result.astype(jnp.bfloat16)


def solution(mesh):
    placed = (
        P("row", "col"),
        P("col"),
        P("row", "col"),
        P("row", None),
        P("row", None),
        P("row", "col"),
    )
    return jax.shard_map(
        local, mesh=mesh, in_specs=placed, out_specs=P("row", "col"), check_vma=False
    )
```

profile of v0, /device:TPU:18, one launch (start us, length us, event | category | flops | bytes accessed | tf_op | source)
XLA Modules:
  0.0 702.7 jit_solution(13769813480248491811)
XLA Ops:
  6.5 1.9 constant_dynamic-slice_fusion
  8.4 0.0 all-gather.10.cloned.1.call-start
  8.5 0.7 convert_element_type.43
  9.2 1.3 fusion.11
  10.4 79.2 %psum.7 = f32[1024]{0:T(1024)S(1)} all-reduce(f32[1024]{0:T(1024)S(1)} %fusion.11), channel_id=1, replica_groups=mesh['row'=4,'col'=32] {'col'}, use_global_device_ids=true, to_apply=%region_1.2 | all-reduce | flops 1024 | bytes 8192 | tf_op jit(solution)/shard_map/psum | solution.py:46
  89.6 2.0 fusion.13
  91.7 1.9 constant_dynamic-slice_fusion.1
  93.7 0.5 all-gather.18.cloned.1.call-update
  94.4 241.9 %all-gather.10.cloned.1.call-done = bf16[1024,8192]{1,0:T(8,128)(2,1)} async-done(((bf16[1024,256]{1,0:T(8,128)(2,1)}), bf16[1024,8192]{1,0:T(8,128)(2,1)}) %all-gather.10.cloned.1.call-update) | async-done | bytes 16777232 | tf_op jit(solution)/shard_map/all_gather | solution.py:51
  336.2 12.0 %fusion.10 = f32[1024,1,128]{0,2,1:T(8,128)S(1)} fusion(bf16[1024,8192]{1,0:T(8,128)(2,1)} %all-gather.10.cloned.1.call-done, bf16[8192,128]{1,0:T(8,128)(2,1)} %all-gather.14.cloned.1.call-done), kind=kOutput, calls=%fused_computation.15 | convolution fusion | flops 2147745792 | bytes 19398656 | tf_op jit(solution)/shard_map/dot_general | solution.py:54
  348.3 1.2 fusion.29
  349.4 0.7 pad_maximum_fusion
  350.2 16.4 %all-gather.12.cloned.1.call-done = bf16[8192,128]{1,0:T(8,128)(2,1)} async-done(((bf16[2048,128]{1,0:T(8,128)(2,1)}), bf16[8192,128]{1,0:T(8,128)(2,1)}) %all-gather.12.cloned.1.call-update) | async-done | bytes 2097168 | tf_op jit(solution)/shard_map/all_gather | solution.py:59
  366.6 12.7 %convolution_convert_fusion.2 = bf16[1024,128]{0,1:T(8,128)(2,1)} fusion(bf16[1024,8192]{1,0:T(8,128)(2,1)} %all-gather.10.cloned.1.call-done, bf16[8192,128]{1,0:T(8,128)(2,1)} %all-gather.12.cloned.1.call-done), kind=kOutput, calls=%fused_computation.13 | convolution fusion | flops 2147614720 | bytes 19136512 | tf_op jit(solution)/shard_map/dot_general | solution.py:54
  379.4 0.7 all-gather.22.cloned.1.call-update
  380.1 0.2 all-gather.20.cloned.1.call-start
  380.4 3.0 multiply_cosine_fusion
  383.3 5.7 iota_compare_fusion
  389.0 17.1 %all-gather.18.cloned.1.call-done = bf16[8192,256]{1,0:T(8,128)(2,1)} async-done(((bf16[2048,256]{1,0:T(8,128)(2,1)}), bf16[8192,256]{1,0:T(8,128)(2,1)}) %all-gather.18.cloned.1.call-update) | async-done | bytes 4194320 | tf_op jit(solution)/shard_map/all_gather | solution.py:56
  406.1 9.3 %fusion.38 = f32[1024,256]{0,1:T(8,128)S(1)} fusion(bf16[1024,8192]{1,0:T(8,128)(2,1)} %all-gather.10.cloned.1.call-done, bf16[8192,256]{1,0:T(8,128)(2,1)} %all-gather.18.cloned.1.call-done), kind=kOutput, calls=%fused_computation.53 | convolution fusion | flops 4294967296 | bytes 22020096 | tf_op jit(solution)/shard_map/dot_general | solution.py:54
  415.5 0.1 fusion.37
  415.5 0.3 copy.13
  415.9 0.3 copy.12
  416.2 2.2 subtract_convert_fusion
  418.4 9.5 %all-gather.16.cloned.1.call-done = bf16[4096,1,128]{0,2,1:T(8,128)(2,1)} async-done(((bf16[1024,1,128]{0,2,1:T(8,128)(2,1)}), bf16[4096,1,128]{0,2,1:T(8,128)(2,1)}) %all-gather.16.cloned.1.call-update) | async-done | bytes 1048592 | tf_op jit(solution)/shard_map/all_gather | solution.py:77
  427.8 1.6 copy.7
  429.5 15.7 %fusion = (f32[1024,2]{0,1:T(2,128)S(1)}, f32[2,4096,1024]{2,1,0:T(8,128)}) fusion(pred[1024,4096]{0,1:T(8,128)(4,1)} %iota_compare_fusion, bf16[1024,2,64]{2,0,1:T(8,128)(2,1)} %get-tuple-element.6, bf16[1024,2,64]{2,0,1:T(8,128)(2,1)S(1)} %get-tuple-element.5, bf16[4096,128]{1,0:T(8,128)(2,1)S(1)} %copy.7), kind=kOutput, calls=%fused_computation.2 | convolution fusion | flops 2173696000 | bytes 39329792 | tf_op jit(solution)/shard_map/qhd,khd->qhk/dot_general | solution.py:84
  445.2 15.1 %fusion.1 = f32[1024,2]{0,1:T(2,128)S(1)} fusion(f32[2,4096,1024]{2,1,0:T(8,128)} %get-tuple-element.14, f32[1024,2]{0,1:T(2,128)S(1)} %broadcast_maximum_fusion, pred[1024,4096]{0,1:T(8,128)(4,1)S(1)} %copy-done), kind=kLoop, calls=%fused_computation.3 | loop fusion | flops 41940992 | bytes 37765120 | tf_op jit(solution)/shard_map/reduce_sum | solution.py:92
  460.3 18.4 %divide_convert_fusion = bf16[1024,2,128]{0,2,1:T(8,128)(2,1)} fusion(f32[1024,2]{0,1:T(2,128)S(1)} %fusion.1, f32[2,4096,1024]{2,1,0:T(8,128)} %get-tuple-element.14, f32[1024,2]{0,1:T(2,128)S(1)} %broadcast_maximum_fusion, pred[1024,4096]{0,1:T(8,128)(4,1)} %iota_compare_fusion, bf16[4096,128]{0,1:T(8,128)(2,1)} %all-gather.24.cloned.1.call-done), kind=kOutput, calls=%fused_computation.20 | convolution fusion | flops 2189950976 | bytes 39337984 | tf_op jit(solution)/shard_map/qhk,khd->qhd/dot_general | solution.py:93
  478.8 10.4 %all-gather.22.cloned.1.call-done = bf16[8192,256]{1,0:T(8,128)(2,1)} async-done(((bf16[2048,256]{1,0:T(8,128)(2,1)}), bf16[8192,256]{1,0:T(8,128)(2,1)}) %all-gather.22.cloned.1.call-update) | async-done | bytes 4194320 | tf_op jit(solution)/shard_map/all_gather | solution.py:103
  489.2 194.4 %all-gather.20.cloned.1.call-done = bf16[1024,8192]{0,1:T(8,128)(2,1)} async-done(((bf16[1024,256]{0,1:T(8,128)(2,1)}), bf16[1024,8192]{0,1:T(8,128)(2,1)}) %all-gather.20.cloned.1.call-update) | async-done | bytes 16777232 | tf_op jit(solution)/shard_map/all_gather | solution.py:100
  683.6 12.3 %convolution_convert_fusion = bf16[1024,256]{1,0:T(8,128)(2,1)} fusion(bf16[1024,8192]{0,1:T(8,128)(2,1)} %all-gather.20.cloned.1.call-done, bf16[8192,256]{1,0:T(8,128)(2,1)} %all-gather.22.cloned.1.call-done), kind=kOutput, calls=%fused_computation.11 | convolution fusion | flops 4295229440 | bytes 21495808 | tf_op jit(solution)/shard_map/dot_general | solution.py:101
  (21 shorter events, 0.4 us)
Async XLA Ops:
  6.5 87.8 %all-gather.14.cloned.1.call-start = ((), (), s32[]{:S(2)}) async-start(), calls=%async_computation.2 | async-start | bytes 2621440 | tf_op jit(solution)/shard_map/all_gather | solution.py:58
  8.4 327.8 %all-gather.10.cloned.1.call-start = ((), (), s32[]{:S(2)}) async-start(), calls=%async_computation | async-start | bytes 17301504 | tf_op jit(solution)/shard_map/all_gather | solution.py:51
  91.7 274.9 %all-gather.12.cloned.1.call-start = ((), (), s32[]{:S(2)}) async-start(), calls=%async_computation.1 | async-start | bytes 2621440 | tf_op jit(solution)/shard_map/all_gather | solution.py:59
  93.7 312.4 %all-gather.18.cloned.1.call-start = ((), (), s32[]{:S(2)}) async-start(), calls=%async_computation.4 | async-start | bytes 5242880 | tf_op jit(solution)/shard_map/all_gather | solution.py:56
  94.3 333.6 %all-gather.16.cloned.1.call-start = ((), (), s32[]{:S(2)}) async-start(), calls=%async_computation.3 | async-start | bytes 1310720 | tf_op jit(solution)/shard_map/all_gather | solution.py:77
  350.2 110.2 %all-gather.24.cloned.1.call-start = ((), (), s32[]{:S(2)}) async-start(), calls=%async_computation.7 | async-start | bytes 1310720 | tf_op jit(solution)/shard_map/all_gather | solution.py:78
  379.4 109.8 %all-gather.22.cloned.1.call-start = ((), (), s32[]{:S(2)}) async-start(), calls=%async_computation.6 | async-start | bytes 5242880 | tf_op jit(solution)/shard_map/all_gather | solution.py:103
  380.1 303.4 %all-gather.20.cloned.1.call-start = ((), (), s32[]{:S(2)}) async-start(), calls=%async_computation.5 | async-start | bytes 17301504 | tf_op jit(solution)/shard_map/all_gather | solution.py:100
  429.4 15.7 %copy-start = (pred[1024,4096]{0,1:T(8,128)(4,1)S(1)}, pred[1024,4096]{0,1:T(8,128)(4,1)}, u32[]{:S(2)}) copy-start(pred[1024,4096]{0,1:T(8,128)(4,1)} %iota_compare_fusion) | copy-start | bytes 12582916
Sparse Core Ops, SparseCore 0:
  9.0 26.3 all-gather.13
  91.8 244.3 all-gather.9
  337.9 28.6 all-gather.11
  368.1 37.9 all-gather.17
  407.6 20.1 all-gather.15
  429.3 20.1 all-gather.23
  451.2 37.9 all-gather.21
  490.8 192.6 all-gather.19
where the time goes:
time: 706 us; the launch traced here: 703 us
  waiting for transfers between devices  491 us (70%)
  matrix products  80.5 us (11%)
  blocking collectives  79.2 us (11%)
  other arithmetic  31.8 us (5%)
  between operations  13.6 us (2%)
    all_gather x1, waiting for transfers between devices, local(): hidden = lax.all_gather(normed, 'col', axis=1, tiled=True)  242 us
    all_gather x1, waiting for transfers between devices, local(): all_heads = lax.all_gather(attended, 'col', axis=1, tiled=True)  194 us
    psum x1, blocking collectives, local(): square_total = lax.psum(jnp.sum(local_wide * local_wide, axis=1), 'col')  79.2 us
    dot_general x3, matrix products, contract(): return jnp.dot(hidden, piece, preferred_element_type=jnp.float32)  34.1 us
    dot_general x1, matrix products, local(): jnp.einsum('qhk,khd->qhd', exponentials.astype(jnp.bfloat16), value_piece...  18.4 us
    all_gather x1, waiting for transfers between devices, local(): query = contract(lax.all_gather(w_query, 'row', axis=0, tiled=True))  17.1 us
    all_gather x1, waiting for transfers between devices, local(): lax.all_gather(value_cols, 'row', axis=0, tiled=True)  16.4 us
    dot_general x1, matrix products, local(): jnp.einsum('qhd,khd->qhk', query_rot, key_piece, preferred_element_type=j...  15.7 us
  transfers between devices with their start and end apart: 8, of which 6 were waited for; matrix products, arithmetic and copies ran while one was open for 15% of the time, Pallas kernels for 0%

commit v1 on v0

v1 whole, which is shorter than its diff:
```python
import functools

import jax
import jax.numpy as jnp
import numpy as np
from jax import lax
from jax.experimental import pallas as pl
from jax.experimental.pallas import tpu as pltpu
from jax.sharding import PartitionSpec as P

MESH = pl.DeviceIdType.MESH
HEAD_DIM = 128
TOK = 1024
B = 256
CHUNKS = TOK // B
LENGTH = 4096
D = 8192
SCALE = HEAD_DIM**-0.5 * 1.4426950408889634
F32 = jnp.float32
BF16 = jnp.bfloat16


def rope_constants():
    half = HEAD_DIM // 2
    frequency = np.exp(-np.log(500000.0) * (np.arange(half) * (2.0 / HEAD_DIM)))
    angles = np.arange(LENGTH)[:, None] * frequency[None, :]
    cos, sin = np.cos(angles), np.sin(angles)
    return (
        np.concatenate([cos, cos], 1).astype(np.float32),
        np.concatenate([-sin, sin], 1).astype(np.float32),
    )


def remote(src, dst, send, recv, device):
    return pltpu.make_async_remote_copy(
        src_ref=src, dst_ref=dst, send_sem=send, recv_sem=recv, device_id=device, device_id_type=MESH
    )


def block(i, size=B):
    return pl.ds(pl.multiple_of(i * size, size), size)


def kernel(
    act, gain, wq, wk, wv, wo, cos_all, sin_all, out,
    a1, a2, w, wkv, wout, stage1, stage2, got1, got2, own1, own2, kv_stage, kv_got, kv_own, kvo, inv, cos, sin, q,
    ss1, ss2,
    loc_sem, ag_s, ag_r, ss_s, ss_r, ssx_s, ssx_r, w_s, w_r, wf_s, wf_r, kvw_s, kvw_r, rs_s, rs_r, kvp_s, kvp_r, kvg_s,
    kvg_r, kvf_s, kvf_r,
):
    row, col = lax.axis_index("row"), lax.axis_index("col")
    yh, co = row // 2, row % 2
    z, yl, x = col // 8, (col // 4) % 2, col % 4
    g = z * 2 + yl

    def at(yh_, co_, z_, yl_, x_):
        return (yh_ * 2 + co_, z_ * 8 + yl_ * 4 + x_)

    z_peers = [at(yh, co, (z + d) % 4, yl, x) for d in (1, 3, 2)]
    yl_peer = at(yh, co, z, 1 - yl, x)
    x_at = [(x + d) % 4 for d in (1, 3, 2)]
    x_peers = [at(yh, co, z, yl, v) for v in x_at]
    far_at = [(x + d) % 4 for d in (2, 1, 3, 0)]
    far_peers = [at(1 - yh, co, z, yl, v) for v in far_at]
    y_peer = at(1 - yh, co, z, yl, x)
    sibling = at(yh, 1 - co, z, yl, x)

    barrier = pltpu.get_barrier_semaphore()
    everyone = z_peers + [yl_peer] + x_peers + far_peers + [sibling]
    for peer in everyone:
        pl.semaphore_signal(barrier, inc=1, device_id=peer, device_id_type=MESH)

    sent = []

    def send(src, dst, s, r, device):
        copy = remote(src, dst, s, r, device)
        copy.start()
        sent.append(copy)

    def arrived(dst, s, r):
        remote(dst, dst, s, r, sibling).wait_recv()

    local = [
        pltpu.make_async_copy(cos_all.at[block(row, TOK)], cos, loc_sem.at[0]),
        pltpu.make_async_copy(sin_all.at[block(row, TOK)], sin, loc_sem.at[1]),
        pltpu.make_async_copy(wk.at[:, x, :, block(g, 128)], wkv.at[pl.ds(2 * row, 2), :, pl.ds(0, 128)], loc_sem.at[2]),
        pltpu.make_async_copy(wv.at[:, x, :, block(g, 128)], wkv.at[pl.ds(2 * row, 2), :, pl.ds(128, 128)], loc_sem.at[3]),
        pltpu.make_async_copy(wq.at[:, x], w.at[pl.ds(2 * row, 2), :, block(x)], loc_sem.at[4]),
        pltpu.make_async_copy(wo.at[:, x], wout.at[pl.ds(2 * row, 2), :, block(x)], loc_sem.at[5]),
    ]
    for copy in local:
        copy.start()
    wide = act[...].astype(F32)
    a1[:, block(g)] = (wide * gain[...].astype(F32)).astype(BF16)
    square = wide * wide
    high = square.astype(BF16)
    low = (square - high.astype(F32)).astype(BF16)
    ones = jnp.ones((8, B), BF16)
    along = (((1,), (1,)), ((), ()))
    sums = lax.dot_general(ones, high, along, preferred_element_type=F32) + lax.dot_general(
        ones, low, along, preferred_element_type=F32
    )
    ss1[g] = sums[0:1]
    kvo[:, 2 * HEAD_DIM :] = jnp.ones((LENGTH, HEAD_DIM), BF16)

    pl.semaphore_wait(barrier, len(everyone))

    def kv_slab(r):
        return wkv.at[pl.ds(2 * r, 2)]

    local[2].wait()
    local[3].wait()
    send(kv_slab(row), kv_slab(row), kvw_s.at[0], kvw_r.at[0], y_peer)
    send(kv_slab(row), kv_slab(row), kvw_s.at[1], kvw_r.at[1], sibling)

    def gather_send(phase, a, t):
        tile = a.at[pl.ds(t * B, B), block(g)]
        for k, peer in enumerate([yl_peer] + z_peers):
            send(tile, tile, ag_s.at[phase, t, k], ag_r.at[phase, t, g], peer)

    def gather_pass(phase, a, t):
        other = z * 2 + 1 - yl
        tile = a.at[pl.ds(t * B, B), block(other)]
        arrived(tile, ag_s.at[phase, t, 0], ag_r.at[phase, t, other])
        for k, peer in enumerate(z_peers):
            send(tile, tile, ag_s.at[phase, t, 4 + k], ag_r.at[phase, t, other], peer)

    def gather_wait(phase, a, t):
        for d in (1, 3, 2):
            for yl_ in range(2):
                who = ((z + d) % 4) * 2 + yl_
                arrived(a.at[pl.ds(t * B, B), block(who)], ag_s.at[phase, t, 0], ag_r.at[phase, t, who])

    def weight_send(phase, src, dst):
        piece = dst.at[pl.ds(2 * row, 2), :, block(x)]
        for k, (xd, peer) in enumerate(zip(far_at, far_peers)):
            send(src.at[:, xd], piece, w_s.at[phase, k], w_r.at[phase, 1, x], peer)
        for k, (xd, peer) in enumerate(zip(x_at, x_peers)):
            send(src.at[:, xd], piece, w_s.at[phase, 4 + k], w_r.at[phase, 0, x], peer)

    far_row = (1 - yh) * 2 + co

    def weight_pass(phase, dst):
        for xs in x_at:
            arrived(dst.at[pl.ds(2 * row, 2), :, block(xs)], w_s.at[phase, 0], w_r.at[phase, 0, xs])
        local[4 + phase].wait()
        slab = dst.at[pl.ds(2 * row, 2)]
        send(slab, slab, wf_s.at[phase, 0], wf_r.at[phase, 0], sibling)
        for xs in far_at:
            arrived(dst.at[pl.ds(2 * far_row, 2), :, block(xs)], w_s.at[phase, 0], w_r.at[phase, 1, xs])
        slab = dst.at[pl.ds(2 * far_row, 2)]
        send(slab, slab, wf_s.at[phase, 1], wf_r.at[phase, 1], sibling)

    def weight_wait(phase, dst):
        arrived(dst.at[pl.ds(2 * (row + 1 - 2 * co), 2)], wf_s.at[phase, 0], wf_r.at[phase, 0])
        arrived(dst.at[pl.ds(2 * (far_row + 1 - 2 * co), 2)], wf_s.at[phase, 1], wf_r.at[phase, 1])

    def partial_send(phase, a, weights, stage, got, own, t):
        rows = pl.ds(t * B, B)
        for k, (xd, peer) in enumerate(zip(x_at, x_peers)):
            part = jnp.dot(
                a[rows, :], weights[:, :, block(xd)].reshape(8 * B, B), preferred_element_type=F32
            )
            stage[k, rows, :] = part.astype(BF16)
            send(stage.at[k, rows], got.at[x, rows], rs_s.at[phase, t, k], rs_r.at[phase, t, x], peer)
        own[rows, :] = jnp.dot(a[rows, :], weights[:, :, block(x)].reshape(8 * B, B), preferred_element_type=F32)

    def partial_sum(phase, got, own, t):
        rows = pl.ds(t * B, B)
        total = own[rows, :]
        for xs in x_at:
            arrived(got.at[xs, rows], rs_s.at[phase, t, 0], rs_r.at[phase, t, xs])
            total = total + got[xs, rows, :].astype(F32)
        return total

    for k, peer in enumerate([yl_peer] + z_peers):
        send(ss1.at[g], ss1.at[g], ss_s.at[k], ss_r.at[g], peer)
    for t in range(CHUNKS):
        gather_send(0, a1, t)
        if t == 0:
            weight_send(0, wq, w)

    arrived(kv_slab(far_row), kvw_s.at[0], kvw_r.at[0])
    send(kv_slab(far_row), kv_slab(far_row), kvw_s.at[2], kvw_r.at[2], sibling)
    arrived(kv_slab(row + 1 - 2 * co), kvw_s.at[1], kvw_r.at[1])

    other = z * 2 + 1 - yl
    arrived(ss1.at[other], ss_s.at[0], ss_r.at[other])
    for k, peer in enumerate(z_peers):
        send(ss1.at[other], ss1.at[other], ss_s.at[4 + k], ss_r.at[other], peer)

    arrived(kv_slab(far_row + 1 - 2 * co), kvw_s.at[2], kvw_r.at[2])

    def kv_copy(t):
        rows = pl.ds(t * B, B)
        return remote(kv_stage.at[rows], kv_got.at[x], kvp_s.at[t], kvp_r.at[x], at(yh, co, z, yl, t))

    def kv_part(t):
        rows = pl.ds(t * B, B)
        part = jnp.dot(a1[rows, :], wkv[...].reshape(8 * B, B), preferred_element_type=F32)
        kv_stage[rows, :] = part.astype(BF16)

        @pl.when(x != t)
        def _():
            kv_copy(t).start()

        @pl.when(x == t)
        def _():
            kv_own[...] = part

    for t in range(CHUNKS):
        gather_pass(0, a1, t)
        gather_wait(0, a1, t)
        kv_part(t)
        if t == 0:
            for d in (1, 3, 2):
                for yl_ in range(2):
                    who = ((z + d) % 4) * 2 + yl_
                    arrived(ss1.at[who], ss_s.at[0], ss_r.at[who])
            ss2[x] = jnp.sum(ss1[...], axis=0)
            for k, peer in enumerate(x_peers):
                send(ss2.at[x], ss2.at[x], ssx_s.at[k], ssx_r.at[x], peer)

    weight_pass(0, w)
    weight_wait(0, w)
    for t in range(CHUNKS):
        partial_send(0, a1, w, stage1, got1, own1, t)
    weight_send(1, wo, wout)

    for xs in x_at:
        arrived(ss2.at[xs], ssx_s.at[0], ssx_r.at[xs])
    factor = lax.rsqrt(jnp.sum(ss2[...], axis=0) / D + 1e-05)
    for b in range(TOK // 128):
        inv[pl.ds(b * 128, 128), :] = jnp.broadcast_to(factor[:, b * 128 : (b + 1) * 128], (128, 128)).T
    local[0].wait()
    local[1].wait()

    mine = block(x)
    total = kv_own[...]
    for xs in x_at:
        arrived(kv_got.at[xs], kvp_s.at[0], kvp_r.at[xs])
        total = total + kv_got[xs].astype(F32)
    scale = inv[mine, :]
    key = total[:, :HEAD_DIM] * scale
    key = (key * cos[mine, :] + pltpu.roll(key, HEAD_DIM // 2, 1) * sin[mine, :]).astype(BF16)
    value = (total[:, HEAD_DIM:] * scale).astype(BF16)
    kvo[block(row * 4 + x), 0 : 2 * HEAD_DIM] = jnp.concatenate([key, value], axis=1)

    def quarter(r, xs):
        return kvo.at[block(r * 4 + xs), pl.ds(0, 2 * HEAD_DIM)]

    def whole(r):
        return kvo.at[block(r, TOK), pl.ds(0, 2 * HEAD_DIM)]

    def kv_down():
        return remote(quarter(row, x), quarter(row, x), kvg_s.at[3], kvg_r.at[row, x], y_peer)

    def kv_across(which, r):
        return remote(whole(r), whole(r), kvf_s.at[which], kvf_r.at[which], sibling)

    @pl.when(yh == 0)
    def _():
        kv_down().start()

    for k, peer in enumerate(x_peers):
        send(quarter(row, x), quarter(row, x), kvg_s.at[k], kvg_r.at[row, x], peer)

    above = row - 2

    def kv_relay():
        return [
            remote(quarter(above, x), quarter(above, x), kvg_s.at[4 + k], kvg_r.at[above, x], peer)
            for k, peer in enumerate(x_peers)
        ]

    @pl.when(yh == 1)
    def _():
        arrived(quarter(above, x), kvg_s.at[0], kvg_r.at[above, x])
        for copy in kv_relay():
            copy.start()

    for xs in x_at:
        arrived(quarter(row, xs), kvg_s.at[0], kvg_r.at[row, xs])

    @pl.when(co == 0)
    def _():
        kv_across(0, row).start()

    @pl.when(yh == 1)
    def _():
        for xs in x_at:
            arrived(quarter(above, xs), kvg_s.at[0], kvg_r.at[above, xs])
        kv_across(1, above).start()
        arrived(whole(above + 1 - 2 * co), kvf_s.at[1], kvf_r.at[1])

    @pl.when(co == 1)
    def _():
        arrived(whole(row - 1), kvf_s.at[0], kvf_r.at[0])

    for t in range(CHUNKS):
        rows = pl.ds(t * B, B)
        total = partial_sum(0, got1, own1, t)
        scale = inv[rows, :] * SCALE
        for h in range(2):
            part = total[:, h * HEAD_DIM : (h + 1) * HEAD_DIM] * scale
            part = part * cos[rows, :] + pltpu.roll(part, HEAD_DIM // 2, 1) * sin[rows, :]
            q[pl.ds(h * B, B), :] = part.astype(BF16)
        width = (t + 1) * B
        here = kvo[pl.ds(pl.multiple_of(row * TOK, TOK), width), :]
        queries = q[...]
        s = lax.dot_general(queries, here[:, :HEAD_DIM], along, preferred_element_type=F32)
        query_at = lax.broadcasted_iota(jnp.int32, s.shape, 0) % B + t * B
        key_at = lax.broadcasted_iota(jnp.int32, s.shape, 1)
        s = jnp.where(key_at <= query_at, s, -1e30)
        top = jnp.max(s, axis=1, keepdims=True)
        p = jnp.exp2(s - top).astype(BF16)
        acc = jnp.dot(p, here[:, HEAD_DIM:], preferred_element_type=F32)

        def step(kb, carry):
            top, acc = carry
            there = kvo[block(kb, TOK), :]
            s = lax.dot_general(q[...], there[:, :HEAD_DIM], along, preferred_element_type=F32)
            new = jnp.maximum(top, jnp.max(s, axis=1, keepdims=True))
            p = jnp.exp2(s - new).astype(BF16)
            acc = acc * jnp.exp2(top - new) + jnp.dot(p, there[:, HEAD_DIM:], preferred_element_type=F32)
            return new, acc

        top, acc = lax.fori_loop(0, row, step, (top, acc))
        mixed = (acc[:, :HEAD_DIM] / acc[:, HEAD_DIM:]).astype(BF16)
        a2[rows, block(g)] = jnp.concatenate([mixed[:B], mixed[B:]], axis=1)
        gather_send(1, a2, t)

    weight_pass(1, wout)
    weight_wait(1, wout)
    for t in range(CHUNKS):
        gather_pass(1, a2, t)
    for t in range(CHUNKS):
        gather_wait(1, a2, t)
        partial_send(1, a2, wout, stage2, got2, own2, t)
    for t in range(CHUNKS):
        out[pl.ds(t * B, B), :] = partial_sum(1, got2, own2, t).astype(BF16)

    for copy in sent:
        copy.wait_send()
    for t in range(CHUNKS):

        @pl.when(x != t)
        def _():
            kv_copy(t).wait_send()

    @pl.when(yh == 0)
    def _():
        kv_down().wait_send()

    @pl.when(yh == 1)
    def _():
        for copy in kv_relay():
            copy.wait_send()
        kv_across(1, above).wait_send()

    @pl.when(co == 0)
    def _():
        kv_across(0, row).wait_send()


def local_step(activations, norm_gain, w_query, w_key, w_value, w_out):
    cos, sin = rope_constants()
    dma = pltpu.SemaphoreType.DMA
    vmem = pl.BlockSpec(memory_space=pltpu.VMEM)
    hbm = pl.BlockSpec(memory_space=pl.ANY)
    return pl.pallas_call(
        kernel,
        out_shape=jax.ShapeDtypeStruct((TOK, B), BF16),
        in_specs=[vmem, vmem] + [hbm] * 6,
        out_specs=vmem,
        scratch_shapes=[
            pltpu.VMEM((TOK, 8 * B), BF16),
            pltpu.VMEM((TOK, 8 * B), BF16),
            pltpu.VMEM((8, B, 4 * B), BF16),
            pltpu.VMEM((8, B, B), BF16),
            pltpu.VMEM((8, B, 4 * B), BF16),
            pltpu.VMEM((3, TOK, B), BF16),
            pltpu.VMEM((3, TOK, B), BF16),
            pltpu.VMEM((4, TOK, B), BF16),
            pltpu.VMEM((4, TOK, B), BF16),
            pltpu.VMEM((TOK, B), F32),
            pltpu.VMEM((TOK, B), F32),
            pltpu.VMEM((TOK, B), BF16),
            pltpu.VMEM((4, B, B), BF16),
            pltpu.VMEM((B, B), F32),
            pltpu.VMEM((LENGTH, 3 * HEAD_DIM), BF16),
            pltpu.VMEM((TOK, 128), F32),
            pltpu.VMEM((TOK, HEAD_DIM), F32),
            pltpu.VMEM((TOK, HEAD_DIM), F32),
            pltpu.VMEM((2 * B, HEAD_DIM), BF16),
            pltpu.VMEM((8, 1, TOK), F32),
            pltpu.VMEM((4, 1, TOK), F32),
            dma((6,)),
            dma((2, CHUNKS, 8)),
            dma((2, CHUNKS, 8)),
            dma((8,)),
            dma((8,)),
            dma((4,)),
            dma((4,)),
            dma((2, 8)),
            dma((2, 2, 4)),
            dma((2, 2)),
            dma((2, 2)),
            dma((3,)),
            dma((3,)),
            dma((2, CHUNKS, 4)),
            dma((2, CHUNKS, 4)),
            dma((CHUNKS,)),
            dma((4,)),
            dma((8,)),
            dma((4, 4)),
            dma((2,)),
            dma((2,)),
        ],
        compiler_params=pltpu.CompilerParams(
            collective_id=0, has_side_effects=True, vmem_limit_bytes=58 * 2**20
        ),
    )(
        activations,
        norm_gain.reshape(1, B),
        w_query.reshape(2, 4, B, B),
        w_key.reshape(2, 4, B, 1024),
        w_value.reshape(2, 4, B, 1024),
        w_out.reshape(2, 4, B, B),
        cos,
        sin,
    )


def solution(mesh):
    placed = (
        P("row", "col"),
        P("col"),
        P("row", "col"),
        P("row", None),
        P("row", None),
        P("row", "col"),
    )
    return jax.shard_map(
        local_step, mesh=mesh, in_specs=placed, out_specs=P("row", "col"), check_vma=False
    )
```

time: 706 us -> 202 us (0.29)
  the two profiles are of different devices: /device:TPU:18 before, /device:TPU:89 now
where the time goes in v1:
time: 202 us
  Pallas kernels  199 us (99%)
  local copies, waits for them, and re-layouts  3.09 us (2%)
    pallas_call x1, Pallas kernels, local_step(): pl.pallas_call(kernel, out_shape=jax.ShapeDtypeStruct((TOK, B), BF16), in...  199 us

profile of v1, /device:TPU:89, one launch (start us, length us, event | category | flops | bytes accessed | tf_op | source)
XLA Modules:
  0.0 202.1 jit_solution(17439250394073834574)
XLA Ops:
  0.0 1.2 reshape.15.gain
  1.2 199.0 %shard_map.82 = bf16[1024,256]{1,0:T(8,128)(2,1)} custom-call(bf16[1024,256]{1,0:T(8,128)(2,1)} %act.1, bf16[1,256]{1,0:T(2,128)(2,1)} %reshape.15.gain, bf16[2,4,256,256]{3,2,1,0:T(8,128)(2,1)} %bitcast.6, bf16[2,4,256,1024]{3,2,1,0:T(8,128)(2,1)} %bitcast.4, bf16[2,4,256,1024]{3,2,1,0:T(8,128)(2,1)} %bitcast.5, bf16[2,4,256,256]{3,2,1,0:T(8,128)(2,1)} %bitcast.7, ...), custom_call_target="tpu_custom_call" | custom-call | tf_op jit(solution)/shard_map/pallas_call | solution.py:371
  200.2 1.9 copy.10

commit v2 on v1

--- a/solution.py
+++ b/solution.py
@@ -45,7 +45,7 @@
     act, gain, wq, wk, wv, wo, cos_all, sin_all, out,
     a1, a2, w, wkv, wout, stage1, stage2, got1, got2, own1, own2, kv_stage, kv_got, kv_own, kvo, inv, cos, sin, q,
     ss1, ss2,
-    loc_sem, ag_s, ag_r, ss_s, ss_r, ssx_s, ssx_r, w_s, w_r, wf_s, wf_r, kvw_s, kvw_r, rs_s, rs_r, kvp_s, kvp_r, kvg_s,
+    loc_sem, agy_s, agy_r, agz_s, agz_r, ss_s, ss_r, ssx_s, ssx_r, w_s, w_r, wf_s, wf_r, kvw_s, kvw_r, rs_s, rs_r, kvp_s, kvp_r, kvg_s,
     kvg_r, kvf_s, kvf_r,
 ):
     row, col = lax.axis_index("row"), lax.axis_index("col")
@@ -60,13 +60,11 @@
     yl_peer = at(yh, co, z, 1 - yl, x)
     x_at = [(x + d) % 4 for d in (1, 3, 2)]
     x_peers = [at(yh, co, z, yl, v) for v in x_at]
-    far_at = [(x + d) % 4 for d in (2, 1, 3, 0)]
-    far_peers = [at(1 - yh, co, z, yl, v) for v in far_at]
     y_peer = at(1 - yh, co, z, yl, x)
     sibling = at(yh, 1 - co, z, yl, x)
 
     barrier = pltpu.get_barrier_semaphore()
-    everyone = z_peers + [yl_peer] + x_peers + far_peers + [sibling]
+    everyone = z_peers + [yl_peer] + x_peers + [y_peer, sibling]
     for peer in everyone:
         pl.semaphore_signal(barrier, inc=1, device_id=peer, device_id_type=MESH)
 
@@ -90,70 +88,93 @@
     ]
     for copy in local:
         copy.start()
-    wide = act[...].astype(F32)
-    a1[:, block(g)] = (wide * gain[...].astype(F32)).astype(BF16)
-    square = wide * wide
-    high = square.astype(BF16)
-    low = (square - high.astype(F32)).astype(BF16)
-    ones = jnp.ones((8, B), BF16)
+    a1[:, block(g)] = (act[...].astype(F32) * gain[...].astype(F32)).astype(BF16)
     along = (((1,), (1,)), ((), ()))
-    sums = lax.dot_general(ones, high, along, preferred_element_type=F32) + lax.dot_general(
-        ones, low, along, preferred_element_type=F32
-    )
-    ss1[g] = sums[0:1]
-    kvo[:, 2 * HEAD_DIM :] = jnp.ones((LENGTH, HEAD_DIM), BF16)
 
     pl.semaphore_wait(barrier, len(everyone))
 
-    def kv_slab(r):
-        return wkv.at[pl.ds(2 * r, 2)]
-
-    local[2].wait()
-    local[3].wait()
-    send(kv_slab(row), kv_slab(row), kvw_s.at[0], kvw_r.at[0], y_peer)
-    send(kv_slab(row), kv_slab(row), kvw_s.at[1], kvw_r.at[1], sibling)
-
-    def gather_send(phase, a, t):
-        tile = a.at[pl.ds(t * B, B), block(g)]
-        for k, peer in enumerate([yl_peer] + z_peers):
-            send(tile, tile, ag_s.at[phase, t, k], ag_r.at[phase, t, g], peer)
-
-    def gather_pass(phase, a, t):
-        other = z * 2 + 1 - yl
-        tile = a.at[pl.ds(t * B, B), block(other)]
-        arrived(tile, ag_s.at[phase, t, 0], ag_r.at[phase, t, other])
-        for k, peer in enumerate(z_peers):
-            send(tile, tile, ag_s.at[phase, t, 4 + k], ag_r.at[phase, t, other], peer)
+    other = z * 2 + 1 - yl
+
+    def tile(a, t, who):
+        return a.at[pl.ds(t * B, B), block(who)]
+
+    def half(a, t, who, h):
+        return a.at[pl.ds(t * B + h * (B // 2), B // 2), block(who)]
+
+    def gather_first(phase, a, t):
+        send(tile(a, t, g), tile(a, t, g), agy_s.at[phase, t], agy_r.at[phase, t], yl_peer)
+
+    def gather_spread(phase, a, t, who, slot):
+        for d, h in ((0, 0), (1, 1), (0, 1), (1, 0)):
+            piece = half(a, t, who, h)
+            send(piece, piece, agz_s.at[phase, t, slot, d * 2 + h], agz_r.at[phase, t, who, d * 2 + h], z_peers[d])
+
+    def gather_second(phase, a, t):
+        arrived(tile(a, t, other), agy_s.at[phase, t], agy_r.at[phase, t])
+        gather_spread(phase, a, t, other, 1)
+
+    def gather_relay(phase, a, t, same):
+        y = yl if same else 1 - yl
+        for d, h, to in ((3, 0, 0), (1, 1, 1)):
+            who = ((z + d) % 4) * 2 + y
+            piece = half(a, t, who, h)
+            arrived(piece, agz_s.at[phase, t, 0, 0], agz_r.at[phase, t, who, to * 3])
+            send(piece, piece, agz_s.at[phase, t, 2, to * 2 + int(same)], agz_r.at[phase, t, who, to * 3], z_peers[to])
 
     def gather_wait(phase, a, t):
-        for d in (1, 3, 2):
-            for yl_ in range(2):
-                who = ((z + d) % 4) * 2 + yl_
-                arrived(a.at[pl.ds(t * B, B), block(who)], ag_s.at[phase, t, 0], ag_r.at[phase, t, who])
-
-    def weight_send(phase, src, dst):
-        piece = dst.at[pl.ds(2 * row, 2), :, block(x)]
-        for k, (xd, peer) in enumerate(zip(far_at, far_peers)):
-            send(src.at[:, xd], piece, w_s.at[phase, k], w_r.at[phase, 1, x], peer)
+        for y in range(2):
+            for d, h, k in ((3, 1, 1), (1, 0, 2), (2, 0, 0), (2, 1, 3)):
+                who = ((z + d) % 4) * 2 + y
+                arrived(half(a, t, who, h), agz_s.at[phase, t, 0, 0], agz_r.at[phase, t, who, k])
+
+    far_row = (1 - yh) * 2 + co
+
+    def weight_piece(dst, r, xs):
+        return dst.at[pl.ds(2 * r, 2), :, block(xs)]
+
+    def weight_first(phase, src, dst):
+        send(src.at[:, x], weight_piece(dst, row, x), w_s.at[phase, 3], w_r.at[phase, 1, x], y_peer)
         for k, (xd, peer) in enumerate(zip(x_at, x_peers)):
-            send(src.at[:, xd], piece, w_s.at[phase, 4 + k], w_r.at[phase, 0, x], peer)
-
-    far_row = (1 - yh) * 2 + co
-
-    def weight_pass(phase, dst):
-        for xs in x_at:
-            arrived(dst.at[pl.ds(2 * row, 2), :, block(xs)], w_s.at[phase, 0], w_r.at[phase, 0, xs])
+            send(src.at[:, xd], weight_piece(dst, row, x), w_s.at[phase, k], w_r.at[phase, 0, x], peer)
+
+    def weight_relay(phase, dst, k):
+        piece = weight_piece(dst, row, x_at[k])
+        arrived(piece, w_s.at[phase, 0], w_r.at[phase, 0, x_at[k]])
+        send(piece, piece, w_s.at[phase, 4 + k], w_r.at[phase, 1, x_at[k]], y_peer)
+
+    def weight_near(phase, dst):
         local[4 + phase].wait()
         slab = dst.at[pl.ds(2 * row, 2)]
         send(slab, slab, wf_s.at[phase, 0], wf_r.at[phase, 0], sibling)
-        for xs in far_at:
-            arrived(dst.at[pl.ds(2 * far_row, 2), :, block(xs)], w_s.at[phase, 0], w_r.at[phase, 1, xs])
-        slab = dst.at[pl.ds(2 * far_row, 2)]
-        send(slab, slab, wf_s.at[phase, 1], wf_r.at[phase, 1], sibling)
+
+    def weight_far(phase, dst):
+        for k, xs in enumerate([x] + x_at):
+            piece = weight_piece(dst, far_row, xs)
+            arrived(piece, w_s.at[phase, 0], w_r.at[phase, 1, xs])
+            send(piece, piece, wf_s.at[phase, 1 + k], wf_r.at[phase, 1 + k], sibling)
 
     def weight_wait(phase, dst):
         arrived(dst.at[pl.ds(2 * (row + 1 - 2 * co), 2)], wf_s.at[phase, 0], wf_r.at[phase, 0])
-        arrived(dst.at[pl.ds(2 * (far_row + 1 - 2 * co), 2)], wf_s.at[phase, 1], wf_r.at[phase, 1])
+        for k, xs in enumerate([x] + x_at):
+            piece = weight_piece(dst, far_row + 1 - 2 * co, xs)
+            arrived(piece, wf_s.at[phase, 1 + k], wf_r.at[phase, 1 + k])
+
+    def kv_slab(r):
+        return wkv.at[pl.ds(2 * r, 2)]
+
+    def kv_weight_first():
+        local[2].wait()
+        local[3].wait()
+        send(kv_slab(row), kv_slab(row), kvw_s.at[0], kvw_r.at[0], y_peer)
+        send(kv_slab(row), kv_slab(row), kvw_s.at[1], kvw_r.at[1], sibling)
+
+    def kv_weight_relay():
+        arrived(kv_slab(far_row), kvw_s.at[0], kvw_r.at[0])
+        send(kv_slab(far_row), kv_slab(far_row), kvw_s.at[2], kvw_r.at[2], sibling)
+
+    def kv_weight_wait():
+        arrived(kv_slab(row + 1 - 2 * co), kvw_s.at[1], kvw_r.at[1])
+        arrived(kv_slab(far_row + 1 - 2 * co), kvw_s.at[2], kvw_r.at[2])
 
     def partial_send(phase, a, weights, stage, got, own, t):
         rows = pl.ds(t * B, B)
@@ -173,23 +194,39 @@
             total = total + got[xs, rows, :].astype(F32)
         return total
 
-    for k, peer in enumerate([yl_peer] + z_peers):
-        send(ss1.at[g], ss1.at[g], ss_s.at[k], ss_r.at[g], peer)
-    for t in range(CHUNKS):
-        gather_send(0, a1, t)
-        if t == 0:
-            weight_send(0, wq, w)
-
-    arrived(kv_slab(far_row), kvw_s.at[0], kvw_r.at[0])
-    send(kv_slab(far_row), kv_slab(far_row), kvw_s.at[2], kvw_r.at[2], sibling)
-    arrived(kv_slab(row + 1 - 2 * co), kvw_s.at[1], kvw_r.at[1])
-
-    other = z * 2 + 1 - yl
-    arrived(ss1.at[other], ss_s.at[0], ss_r.at[other])
-    for k, peer in enumerate(z_peers):
-        send(ss1.at[other], ss1.at[other], ss_s.at[4 + k], ss_r.at[other], peer)
-
-    arrived(kv_slab(far_row + 1 - 2 * co), kvw_s.at[2], kvw_r.at[2])
+    def squares_first():
+        wide = act[...].astype(F32)
+        square = wide * wide
+        high = square.astype(BF16)
+        low = (square - high.astype(F32)).astype(BF16)
+        ones = jnp.ones((8, B), BF16)
+        sums = lax.dot_general(ones, high, along, preferred_element_type=F32) + lax.dot_general(
+            ones, low, along, preferred_element_type=F32
+        )
+        ss1[g] = sums[0:1]
+        for k, peer in enumerate([yl_peer] + z_peers):
+            send(ss1.at[g], ss1.at[g], ss_s.at[k], ss_r.at[g], peer)
+
+    def squares_relay():
+        arrived(ss1.at[other], ss_s.at[0], ss_r.at[other])
+        for k, peer in enumerate(z_peers):
+            send(ss1.at[other], ss1.at[other], ss_s.at[4 + k], ss_r.at[other], peer)
+
+    def squares_second():
+        for d in (1, 3, 2):
+            for y in range(2):
+                who = ((z + d) % 4) * 2 + y
+                arrived(ss1.at[who], ss_s.at[0], ss_r.at[who])
+        ss2[x] = jnp.sum(ss1[...], axis=0)
+        for k, peer in enumerate(x_peers):
+            send(ss2.at[x], ss2.at[x], ssx_s.at[k], ssx_r.at[x], peer)
+
+    def squares_wait():
+        for xs in x_at:
+            arrived(ss2.at[xs], ssx_s.at[0], ssx_r.at[xs])
+        factor = lax.rsqrt(jnp.sum(ss2[...], axis=0) / D + 1e-05)
+        for b in range(TOK // 128):
+            inv[pl.ds(b * 128, 128), :] = jnp.broadcast_to(factor[:, b * 128 : (b + 1) * 128], (128, 128)).T
 
     def kv_copy(t):
         rows = pl.ds(t * B, B)
@@ -208,30 +245,52 @@
         def _():
             kv_own[...] = part
 
+    gather_first(0, a1, 0)
+    gather_spread(0, a1, 0, g, 0)
+    weight_first(0, wq, w)
+    gather_first(0, a1, 1)
+    gather_spread(0, a1, 1, g, 0)
+    kv_weight_first()
+    for t in (2, 3):
+        gather_first(0, a1, t)
+        gather_spread(0, a1, t, g, 0)
+    squares_first()
+    kvo[:, 2 * HEAD_DIM :] = jnp.ones((LENGTH, HEAD_DIM), BF16)
+
     for t in range(CHUNKS):
-        gather_pass(0, a1, t)
-        gather_wait(0, a1, t)
-        kv_part(t)
+        gather_second(0, a1, t)
+        gather_relay(0, a1, t, True)
         if t == 0:
-            for d in (1, 3, 2):
-                for yl_ in range(2):
-                    who = ((z + d) % 4) * 2 + yl_
-                    arrived(ss1.at[who], ss_s.at[0], ss_r.at[who])
-            ss2[x] = jnp.sum(ss1[...], axis=0)
-            for k, peer in enumerate(x_peers):
-                send(ss2.at[x], ss2.at[x], ssx_s.at[k], ssx_r.at[x], peer)
-
-    weight_pass(0, w)
+            weight_relay(0, w, 0)
+            weight_relay(0, w, 1)
+            squares_relay()
+        if t == 1:
+            weight_relay(0, w, 2)
+            weight_near(0, w)
+            kv_weight_relay()
+            weight_first(1, wo, wout)
+            squares_second()
+        if t >= 1:
+            gather_relay(0, a1, t - 1, False)
+        if t == 2:
+            kv_weight_wait()
+        if t >= 2:
+            gather_wait(0, a1, t - 2)
+            kv_part(t - 2)
+    gather_relay(0, a1, 3, False)
+    gather_wait(0, a1, 2)
+    kv_part(2)
+    weight_far(0, w)
     weight_wait(0, w)
-    for t in range(CHUNKS):
-        partial_send(0, a1, w, stage1, got1, own1, t)
-    weight_send(1, wo, wout)
-
-    for xs in x_at:
-        arrived(ss2.at[xs], ssx_s.at[0], ssx_r.at[xs])
-    factor = lax.rsqrt(jnp.sum(ss2[...], axis=0) / D + 1e-05)
-    for b in range(TOK // 128):
-        inv[pl.ds(b * 128, 128), :] = jnp.broadcast_to(factor[:, b * 128 : (b + 1) * 128], (128, 128)).T
+    partial_send(0, a1, w, stage1, got1, own1, 0)
+    gather_wait(0, a1, 3)
+    kv_part(3)
+    partial_send(0, a1, w, stage1, got1, own1, 1)
+    for k in range(3):
+        weight_relay(1, wout, k)
+    weight_near(1, wout)
+    squares_wait()
+    partial_send(0, a1, w, stage1, got1, own1, 2)
     local[0].wait()
     local[1].wait()
 
@@ -279,6 +338,7 @@
         for copy in kv_relay():
             copy.start()
 
+    partial_send(0, a1, w, stage1, got1, own1, 3)
     for xs in x_at:
         arrived(quarter(row, xs), kvg_s.at[0], kvg_r.at[row, xs])
 
@@ -328,15 +388,26 @@
         top, acc = lax.fori_loop(0, row, step, (top, acc))
         mixed = (acc[:, :HEAD_DIM] / acc[:, HEAD_DIM:]).astype(BF16)
         a2[rows, block(g)] = jnp.concatenate([mixed[:B], mixed[B:]], axis=1)
-        gather_send(1, a2, t)
-
-    weight_pass(1, wout)
+        gather_first(1, a2, t)
+        gather_spread(1, a2, t, g, 0)
+        if t >= 1:
+            gather_second(1, a2, t - 1)
+            gather_relay(1, a2, t - 1, True)
+        if t >= 2:
+            gather_relay(1, a2, t - 2, False)
+
+    gather_second(1, a2, 3)
+    gather_relay(1, a2, 3, True)
+    gather_relay(1, a2, 2, False)
+    weight_far(1, wout)
     weight_wait(1, wout)
+    gather_wait(1, a2, 0)
+    partial_send(1, a2, wout, stage2, got2, own2, 0)
+    gather_relay(1, a2, 3, False)
     for t in range(CHUNKS):
-        gather_pass(1, a2, t)
-    for t in range(CHUNKS):
-        gather_wait(1, a2, t)
-        partial_send(1, a2, wout, stage2, got2, own2, t)
+        if t >= 1:
+            gather_wait(1, a2, t)
+            partial_send(1, a2, wout, stage2, got2, own2, t)
     for t in range(CHUNKS):
         out[pl.ds(t * B, B), :] = partial_sum(1, got2, own2, t).astype(BF16)
 
@@ -396,16 +467,18 @@
             pltpu.VMEM((8, 1, TOK), F32),
             pltpu.VMEM((4, 1, TOK), F32),
             dma((6,)),
-            dma((2, CHUNKS, 8)),
-            dma((2, CHUNKS, 8)),
+            dma((2, CHUNKS)),
+            dma((2, CHUNKS)),
+            dma((2, CHUNKS, 3, 4)),
+            dma((2, CHUNKS, 8, 4)),
             dma((8,)),
             dma((8,)),
             dma((4,)),
             dma((4,)),
             dma((2, 8)),
             dma((2, 2, 4)),
-            dma((2, 2)),
-            dma((2, 2)),
+            dma((2, 5)),
+            dma((2, 5)),
             dma((3,)),
             dma((3,)),
             dma((2, CHUNKS, 4)),

time: 202 us -> 162 us (0.80)
  the two profiles are of different devices: /device:TPU:89 before, /device:TPU:18 now
where the time goes in v2:
time: 162 us; the launch traced here: 161 us
  Pallas kernels  158 us (98%)
  local copies, waits for them, and re-layouts  3.09 us (2%)
    pallas_call x1, Pallas kernels, local_step(): pl.pallas_call(kernel, out_shape=jax.ShapeDtypeStruct((TOK, B), BF16), in...  158 us

profile of v2, /device:TPU:18, one launch (start us, length us, event | category | flops | bytes accessed | tf_op | source)
XLA Modules:
  0.0 161.5 jit_solution(10957035304340261485)
XLA Ops:
  0.0 1.2 reshape.15.gain
  1.2 158.4 %shard_map.82 = bf16[1024,256]{1,0:T(8,128)(2,1)} custom-call(bf16[1024,256]{1,0:T(8,128)(2,1)} %act.1, bf16[1,256]{1,0:T(2,128)(2,1)} %reshape.15.gain, bf16[2,4,256,256]{3,2,1,0:T(8,128)(2,1)} %bitcast.6, bf16[2,4,256,1024]{3,2,1,0:T(8,128)(2,1)} %bitcast.4, bf16[2,4,256,1024]{3,2,1,0:T(8,128)(2,1)} %bitcast.5, bf16[2,4,256,256]{3,2,1,0:T(8,128)(2,1)} %bitcast.7, ...), custom_call_target="tpu_custom_call" | custom-call | tf_op jit(solution)/shard_map/pallas_call | solution.py:442
  159.6 1.9 %copy.10 = bf16[1024,256]{1,0:T(8,128)(2,1)} copy(bf16[1024,256]{1,0:T(8,128)(2,1)} %shard_map.82) | data formatting | bytes 1048576

commit v3 on v2

--- a/solution.py
+++ b/solution.py
@@ -13,6 +13,7 @@
 TOK = 1024
 B = 256
 CHUNKS = TOK // B
+SUB = B // 4
 LENGTH = 4096
 D = 8192
 SCALE = HEAD_DIM**-0.5 * 1.4426950408889634
@@ -91,6 +92,17 @@
     a1[:, block(g)] = (act[...].astype(F32) * gain[...].astype(F32)).astype(BF16)
     along = (((1,), (1,)), ((), ()))
 
+    wide = act[...].astype(F32)
+    square = wide * wide
+    high = square.astype(BF16)
+    low = (square - high.astype(F32)).astype(BF16)
+    ones = jnp.ones((8, B), BF16)
+    sums = lax.dot_general(ones, high, along, preferred_element_type=F32) + lax.dot_general(
+        ones, low, along, preferred_element_type=F32
+    )
+    ss1[g] = sums[0:1]
+    kvo[:, 2 * HEAD_DIM :] = jnp.ones((LENGTH, HEAD_DIM), BF16)
+
     pl.semaphore_wait(barrier, len(everyone))
 
     other = z * 2 + 1 - yl
@@ -133,9 +145,11 @@
         return dst.at[pl.ds(2 * r, 2), :, block(xs)]
 
     def weight_first(phase, src, dst):
-        send(src.at[:, x], weight_piece(dst, row, x), w_s.at[phase, 3], w_r.at[phase, 1, x], y_peer)
         for k, (xd, peer) in enumerate(zip(x_at, x_peers)):
             send(src.at[:, xd], weight_piece(dst, row, x), w_s.at[phase, k], w_r.at[phase, 0, x], peer)
+
+    def weight_down(phase, src, dst):
+        send(src.at[:, x], weight_piece(dst, row, x), w_s.at[phase, 3], w_r.at[phase, 1, x], y_peer)
 
     def weight_relay(phase, dst, k):
         piece = weight_piece(dst, row, x_at[k])
@@ -176,15 +190,28 @@
         arrived(kv_slab(row + 1 - 2 * co), kvw_s.at[1], kvw_r.at[1])
         arrived(kv_slab(far_row + 1 - 2 * co), kvw_s.at[2], kvw_r.at[2])
 
+    def partial_one(a, weights, t, xd):
+        return jnp.dot(
+            a[pl.ds(t * B, B), :], weights[:, :, block(xd)].reshape(8 * B, B), preferred_element_type=F32
+        )
+
+    def partial_copy(phase, stage, got, t, k):
+        rows = pl.ds(t * B, B)
+        send(stage.at[k, rows], got.at[x, rows], rs_s.at[phase, t, k], rs_r.at[phase, t, x], x_peers[k])
+
+    def partial_make(phase, a, weights, stage, got, own, t):
+        rows = pl.ds(t * B, B)
+        for k, xd in enumerate(x_at):
+            stage[k, rows, :] = partial_one(a, weights, t, xd).astype(BF16)
+        own[rows, :] = partial_one(a, weights, t, x)
+
+    def partial_start(phase, stage, got, t):
+        for k in range(3):
+            partial_copy(phase, stage, got, t, k)
+
     def partial_send(phase, a, weights, stage, got, own, t):
-        rows = pl.ds(t * B, B)
-        for k, (xd, peer) in enumerate(zip(x_at, x_peers)):
-            part = jnp.dot(
-                a[rows, :], weights[:, :, block(xd)].reshape(8 * B, B), preferred_element_type=F32
-            )
-            stage[k, rows, :] = part.astype(BF16)
-            send(stage.at[k, rows], got.at[x, rows], rs_s.at[phase, t, k], rs_r.at[phase, t, x], peer)
-        own[rows, :] = jnp.dot(a[rows, :], weights[:, :, block(x)].reshape(8 * B, B), preferred_element_type=F32)
+        partial_make(phase, a, weights, stage, got, own, t)
+        partial_start(phase, stage, got, t)
 
     def partial_sum(phase, got, own, t):
         rows = pl.ds(t * B, B)
@@ -195,15 +222,6 @@
         return total
 
     def squares_first():
-        wide = act[...].astype(F32)
-        square = wide * wide
-        high = square.astype(BF16)
-        low = (square - high.astype(F32)).astype(BF16)
-        ones = jnp.ones((8, B), BF16)
-        sums = lax.dot_general(ones, high, along, preferred_element_type=F32) + lax.dot_general(
-            ones, low, along, preferred_element_type=F32
-        )
-        ss1[g] = sums[0:1]
         for k, peer in enumerate([yl_peer] + z_peers):
             send(ss1.at[g], ss1.at[g], ss_s.at[k], ss_r.at[g], peer)
 
@@ -228,134 +246,152 @@
         for b in range(TOK // 128):
             inv[pl.ds(b * 128, 128), :] = jnp.broadcast_to(factor[:, b * 128 : (b + 1) * 128], (128, 128)).T
 
-    def kv_copy(t):
-        rows = pl.ds(t * B, B)
-        return remote(kv_stage.at[rows], kv_got.at[x], kvp_s.at[t], kvp_r.at[x], at(yh, co, z, yl, t))
+    above = row - 2
 
     def kv_part(t):
         rows = pl.ds(t * B, B)
         part = jnp.dot(a1[rows, :], wkv[...].reshape(8 * B, B), preferred_element_type=F32)
         kv_stage[rows, :] = part.astype(BF16)
-
-        @pl.when(x != t)
+        kv_own[t] = part
+        for k, xd in enumerate(x_at):
+            piece = kv_stage.at[pl.ds(pl.multiple_of(t * B + xd * SUB, SUB), SUB)]
+            send(piece, kv_got.at[t, x], kvp_s.at[t, k], kvp_r.at[t, x], x_peers[k])
+
+    def kv_piece(r, t, xs):
+        return kvo.at[pl.ds(pl.multiple_of(r * TOK + t * B + xs * SUB, SUB), SUB), pl.ds(0, 2 * HEAD_DIM)]
+
+    def kv_down(t):
+        return remote(kv_piece(row, t, x), kv_piece(row, t, x), kvg_s.at[t, 3], kvg_r.at[1, t, x], y_peer)
+
+    def kv_reduce(t):
+        total = kv_own[t, block(x, SUB), :]
+        for k, xs in enumerate(x_at):
+            arrived(kv_got.at[t, xs], kvp_s.at[t, k], kvp_r.at[t, xs])
+            total = total + kv_got[t, xs].astype(F32)
+        mine = pl.ds(pl.multiple_of(t * B + x * SUB, SUB), SUB)
+        scale = inv[mine, :]
+        key = total[:, :HEAD_DIM] * scale
+        key = (key * cos[mine, :] + pltpu.roll(key, HEAD_DIM // 2, 1) * sin[mine, :]).astype(BF16)
+        value = (total[:, HEAD_DIM:] * scale).astype(BF16)
+        kvo[pl.ds(pl.multiple_of(row * TOK + t * B + x * SUB, SUB), SUB), 0 : 2 * HEAD_DIM] = jnp.concatenate(
+            [key, value], axis=1
+        )
+
+        @pl.when(yh == 0)
         def _():
-            kv_copy(t).start()
-
-        @pl.when(x == t)
+            kv_down(t).start()
+
+        for k, peer in enumerate(x_peers):
+            send(kv_piece(row, t, x), kv_piece(row, t, x), kvg_s.at[t, k], kvg_r.at[0, t, x], peer)
+
+    def kv_relay_copies(t):
+        piece = kv_piece(above, t, x)
+        return [remote(piece, piece, kvg_s.at[t, 4 + k], kvg_r.at[1, t, x], peer) for k, peer in enumerate(x_peers)]
+
+    def kv_relay(t):
+        @pl.when(yh == 1)
         def _():
-            kv_own[...] = part
+            arrived(kv_piece(above, t, x), kvg_s.at[t, 0], kvg_r.at[1, t, x])
+            for copy in kv_relay_copies(t):
+                copy.start()
+
+    def kv_whole(r):
+        return kvo.at[block(r, TOK), pl.ds(0, 2 * HEAD_DIM)]
+
+    def kv_across(which, r):
+        return remote(kv_whole(r), kv_whole(r), kvf_s.at[which], kvf_r.at[which], sibling)
+
+    def kv_own_wait():
+        for t in range(CHUNKS):
+            for xs in x_at:
+                arrived(kv_piece(row, t, xs), kvg_s.at[t, 0], kvg_r.at[0, t, xs])
+
+        @pl.when(co == 0)
+        def _():
+            kv_across(0, row).start()
+
+    def kv_rest_wait():
+        @pl.when(yh == 1)
+        def _():
+            for t in range(CHUNKS):
+                for xs in x_at:
+                    arrived(kv_piece(above, t, xs), kvg_s.at[t, 0], kvg_r.at[1, t, xs])
+            kv_across(1, above).start()
+            arrived(kv_whole(above + 1 - 2 * co), kvf_s.at[1], kvf_r.at[1])
+
+        @pl.when(co == 1)
+        def _():
+            arrived(kv_whole(row - 1), kvf_s.at[0], kvf_r.at[0])
 
     gather_first(0, a1, 0)
+    squares_first()
     gather_spread(0, a1, 0, g, 0)
-    weight_first(0, wq, w)
     gather_first(0, a1, 1)
     gather_spread(0, a1, 1, g, 0)
+    weight_first(0, wq, w)
     kv_weight_first()
-    for t in (2, 3):
-        gather_first(0, a1, t)
-        gather_spread(0, a1, t, g, 0)
-    squares_first()
-    kvo[:, 2 * HEAD_DIM :] = jnp.ones((LENGTH, HEAD_DIM), BF16)
-
-    for t in range(CHUNKS):
-        gather_second(0, a1, t)
-        gather_relay(0, a1, t, True)
-        if t == 0:
-            weight_relay(0, w, 0)
-            weight_relay(0, w, 1)
-            squares_relay()
-        if t == 1:
-            weight_relay(0, w, 2)
-            weight_near(0, w)
-            kv_weight_relay()
-            weight_first(1, wo, wout)
-            squares_second()
-        if t >= 1:
-            gather_relay(0, a1, t - 1, False)
-        if t == 2:
-            kv_weight_wait()
-        if t >= 2:
-            gather_wait(0, a1, t - 2)
-            kv_part(t - 2)
+    gather_first(0, a1, 2)
+    gather_first(0, a1, 3)
+    weight_down(0, wq, w)
+    weight_first(1, wo, wout)
+
+    def gather_turn(phase, a, t):
+        gather_second(phase, a, t)
+        gather_relay(phase, a, t, True)
+        gather_relay(phase, a, t, False)
+
+    gather_second(0, a1, 0)
+    squares_relay()
+    gather_relay(0, a1, 0, True)
+    gather_relay(0, a1, 0, False)
+    gather_spread(0, a1, 2, g, 0)
+    weight_relay(0, w, 0)
+    weight_relay(0, w, 1)
+
+    gather_turn(0, a1, 1)
+    gather_spread(0, a1, 3, g, 0)
+    kv_weight_relay()
+    weight_relay(0, w, 2)
+    weight_near(0, w)
+    squares_second()
+
+    gather_second(0, a1, 2)
+    gather_relay(0, a1, 2, True)
+    kv_weight_wait()
+    gather_wait(0, a1, 0)
+    kv_part(0)
+    gather_relay(0, a1, 2, False)
+
+    gather_second(0, a1, 3)
+    gather_relay(0, a1, 3, True)
+    gather_wait(0, a1, 1)
+    kv_part(1)
+    local[0].wait()
+    local[1].wait()
+    squares_wait()
+    kv_reduce(0)
     gather_relay(0, a1, 3, False)
+
     gather_wait(0, a1, 2)
     kv_part(2)
+    kv_reduce(1)
+    gather_wait(0, a1, 3)
+    kv_part(3)
+    kv_reduce(2)
+    kv_reduce(3)
+    for t in range(3):
+        kv_relay(t)
+
     weight_far(0, w)
     weight_wait(0, w)
-    partial_send(0, a1, w, stage1, got1, own1, 0)
-    gather_wait(0, a1, 3)
-    kv_part(3)
-    partial_send(0, a1, w, stage1, got1, own1, 1)
-    for k in range(3):
-        weight_relay(1, wout, k)
-    weight_near(1, wout)
-    squares_wait()
-    partial_send(0, a1, w, stage1, got1, own1, 2)
-    local[0].wait()
-    local[1].wait()
-
-    mine = block(x)
-    total = kv_own[...]
-    for xs in x_at:
-        arrived(kv_got.at[xs], kvp_s.at[0], kvp_r.at[xs])
-        total = total + kv_got[xs].astype(F32)
-    scale = inv[mine, :]
-    key = total[:, :HEAD_DIM] * scale
-    key = (key * cos[mine, :] + pltpu.roll(key, HEAD_DIM // 2, 1) * sin[mine, :]).astype(BF16)
-    value = (total[:, HEAD_DIM:] * scale).astype(BF16)
-    kvo[block(row * 4 + x), 0 : 2 * HEAD_DIM] = jnp.concatenate([key, value], axis=1)
-
-    def quarter(r, xs):
-        return kvo.at[block(r * 4 + xs), pl.ds(0, 2 * HEAD_DIM)]
-
-    def whole(r):
-        return kvo.at[block(r, TOK), pl.ds(0, 2 * HEAD_DIM)]
-
-    def kv_down():
-        return remote(quarter(row, x), quarter(row, x), kvg_s.at[3], kvg_r.at[row, x], y_peer)
-
-    def kv_across(which, r):
-        return remote(whole(r), whole(r), kvf_s.at[which], kvf_r.at[which], sibling)
-
-    @pl.when(yh == 0)
-    def _():
-        kv_down().start()
-
-    for k, peer in enumerate(x_peers):
-        send(quarter(row, x), quarter(row, x), kvg_s.at[k], kvg_r.at[row, x], peer)
-
-    above = row - 2
-
-    def kv_relay():
-        return [
-            remote(quarter(above, x), quarter(above, x), kvg_s.at[4 + k], kvg_r.at[above, x], peer)
-            for k, peer in enumerate(x_peers)
-        ]
-
-    @pl.when(yh == 1)
-    def _():
-        arrived(quarter(above, x), kvg_s.at[0], kvg_r.at[above, x])
-        for copy in kv_relay():
-            copy.start()
-
-    partial_send(0, a1, w, stage1, got1, own1, 3)
-    for xs in x_at:
-        arrived(quarter(row, xs), kvg_s.at[0], kvg_r.at[row, xs])
-
-    @pl.when(co == 0)
-    def _():
-        kv_across(0, row).start()
-
-    @pl.when(yh == 1)
-    def _():
-        for xs in x_at:
-            arrived(quarter(above, xs), kvg_s.at[0], kvg_r.at[above, xs])
-        kv_across(1, above).start()
-        arrived(whole(above + 1 - 2 * co), kvf_s.at[1], kvf_r.at[1])
-
-    @pl.when(co == 1)
-    def _():
-        arrived(whole(row - 1), kvf_s.at[0], kvf_r.at[0])
+    partial_make(0, a1, w, stage1, got1, own1, 0)
+    kv_relay(3)
+    partial_start(0, stage1, got1, 0)
+    weight_down(1, wo, wout)
+    weight_relay(1, wout, 0)
+    for t in range(1, CHUNKS):
+        partial_make(0, a1, w, stage1, got1, own1, t)
+    kv_own_wait()
 
     for t in range(CHUNKS):
         rows = pl.ds(t * B, B)
@@ -376,6 +412,11 @@
         p = jnp.exp2(s - top).astype(BF16)
         acc = jnp.dot(p, here[:, HEAD_DIM:], preferred_element_type=F32)
 
+        if t == 0:
+            kv_rest_wait()
+            for v in range(1, CHUNKS):
+                partial_start(0, stage1, got1, v)
+
         def step(kb, carry):
             top, acc = carry
             there = kvo[block(kb, TOK), :]
@@ -390,43 +431,49 @@
         a2[rows, block(g)] = jnp.concatenate([mixed[:B], mixed[B:]], axis=1)
         gather_first(1, a2, t)
         gather_spread(1, a2, t, g, 0)
+        if t == 0:
+            weight_relay(1, wout, 1)
+        if t == 1:
+            weight_relay(1, wout, 2)
+            weight_near(1, wout)
+        if t == 2:
+            gather_relay(1, a2, 0, False)
         if t >= 1:
             gather_second(1, a2, t - 1)
             gather_relay(1, a2, t - 1, True)
-        if t >= 2:
-            gather_relay(1, a2, t - 2, False)
-
-    gather_second(1, a2, 3)
-    gather_relay(1, a2, 3, True)
-    gather_relay(1, a2, 2, False)
+
+    gather_relay(1, a2, 1, False)
     weight_far(1, wout)
     weight_wait(1, wout)
     gather_wait(1, a2, 0)
     partial_send(1, a2, wout, stage2, got2, own2, 0)
+    gather_second(1, a2, 3)
+    gather_relay(1, a2, 2, False)
+    gather_relay(1, a2, 3, True)
+    gather_wait(1, a2, 1)
+    partial_send(1, a2, wout, stage2, got2, own2, 1)
     gather_relay(1, a2, 3, False)
-    for t in range(CHUNKS):
-        if t >= 1:
-            gather_wait(1, a2, t)
-            partial_send(1, a2, wout, stage2, got2, own2, t)
-    for t in range(CHUNKS):
+    gather_wait(1, a2, 2)
+    partial_send(1, a2, wout, stage2, got2, own2, 2)
+    out[pl.ds(0, B), :] = partial_sum(1, got2, own2, 0).astype(BF16)
+    gather_wait(1, a2, 3)
+    partial_send(1, a2, wout, stage2, got2, own2, 3)
+    for t in range(1, CHUNKS):
         out[pl.ds(t * B, B), :] = partial_sum(1, got2, own2, t).astype(BF16)
 
     for copy in sent:
         copy.wait_send()
-    for t in range(CHUNKS):
-
-        @pl.when(x != t)
-        def _():
-            kv_copy(t).wait_send()
 
     @pl.when(yh == 0)
     def _():
-        kv_down().wait_send()
+        for t in range(CHUNKS):
+            kv_down(t).wait_send()
 
     @pl.when(yh == 1)
     def _():
-        for copy in kv_relay():
-            copy.wait_send()
+        for t in range(CHUNKS):
+            for copy in kv_relay_copies(t):
+                copy.wait_send()
         kv_across(1, above).wait_send()
 
     @pl.when(co == 0)
@@ -457,8 +504,8 @@
             pltpu.VMEM((TOK, B), F32),
             pltpu.VMEM((TOK, B), F32),
             pltpu.VMEM((TOK, B), BF16),
-            pltpu.VMEM((4, B, B), BF16),
-            pltpu.VMEM((B, B), F32),
+            pltpu.VMEM((CHUNKS, 4, SUB, B), BF16),
+            pltpu.VMEM((CHUNKS, B, B), F32),
             pltpu.VMEM((LENGTH, 3 * HEAD_DIM), BF16),
             pltpu.VMEM((TOK, 128), F32),
             pltpu.VMEM((TOK, HEAD_DIM), F32),
@@ -483,10 +530,10 @@
             dma((3,)),
             dma((2, CHUNKS, 4)),
             dma((2, CHUNKS, 4)),
-            dma((CHUNKS,)),
-            dma((4,)),
-            dma((8,)),
-            dma((4, 4)),
+            dma((CHUNKS, 4)),
+            dma((CHUNKS, 4)),
+            dma((CHUNKS, 8)),
+            dma((2, CHUNKS, 4)),
             dma((2,)),
             dma((2,)),
         ],

time: 162 us -> 133 us (0.82)
  Pallas kernels: 158 us -> 128 us
    pallas_call x1, Pallas kernels: 158 us -> 128 us  [local_step(): pl.pallas_call(kernel, out_shape=jax.ShapeDtypeStruct((TOK, B), BF16), in...]
where the time goes in v3:
time: 133 us; the launch traced here: 131 us
  Pallas kernels  128 us (96%)
  local copies, waits for them, and re-layouts  3.09 us (2%)
    pallas_call x1, Pallas kernels, local_step(): pl.pallas_call(kernel, out_shape=jax.ShapeDtypeStruct((TOK, B), BF16), in...  128 us

profile of v3, /device:TPU:18, one launch (start us, length us, event | category | flops | bytes accessed | tf_op | source)
XLA Modules:
  0.0 131.4 jit_solution(3079129066566812661)
XLA Ops:
  0.0 1.2 reshape.15.gain
  1.2 128.3 %shard_map.82 = bf16[1024,256]{1,0:T(8,128)(2,1)} custom-call(bf16[1024,256]{1,0:T(8,128)(2,1)} %act.1, bf16[1,256]{1,0:T(2,128)(2,1)} %reshape.15.gain, bf16[2,4,256,256]{3,2,1,0:T(8,128)(2,1)} %bitcast.6, bf16[2,4,256,1024]{3,2,1,0:T(8,128)(2,1)} %bitcast.4, bf16[2,4,256,1024]{3,2,1,0:T(8,128)(2,1)} %bitcast.5, bf16[2,4,256,256]{3,2,1,0:T(8,128)(2,1)} %bitcast.7, ...), custom_call_target="tpu_custom_call" | custom-call | tf_op jit(solution)/shard_map/pallas_call | solution.py:489
  129.5 1.9 %copy.10 = bf16[1024,256]{1,0:T(8,128)(2,1)} copy(bf16[1024,256]{1,0:T(8,128)(2,1)} %shard_map.82) | data formatting | bytes 1048576

commit v4 on v3

--- a/solution.py
+++ b/solution.py
@@ -13,6 +13,8 @@
 TOK = 1024
 B = 256
 CHUNKS = TOK // B
+HB = B // 2
+TURNS = TOK // HB
 SUB = B // 4
 LENGTH = 4096
 D = 8192
@@ -89,7 +91,7 @@
     ]
     for copy in local:
         copy.start()
-    a1[:, block(g)] = (act[...].astype(F32) * gain[...].astype(F32)).astype(BF16)
+    a1[:, block(g)] = (act[...].astype(F32) * gain[...].astype(F32).reshape(1, B)).astype(BF16)
     along = (((1,), (1,)), ((), ()))
 
     wide = act[...].astype(F32)
@@ -107,29 +109,31 @@
 
     other = z * 2 + 1 - yl
 
-    def tile(a, t, who):
-        return a.at[pl.ds(t * B, B), block(who)]
-
-    def half(a, t, who, h):
-        return a.at[pl.ds(t * B + h * (B // 2), B // 2), block(who)]
+    def tile(phase, a, t, who):
+        size = HB if phase else B
+        return a.at[pl.ds(t * size, size), block(who)]
+
+    def half(phase, a, t, who, h):
+        size = HB // 2 if phase else B // 2
+        return a.at[pl.ds((2 * t + h) * size, size), block(who)]
 
     def gather_first(phase, a, t):
-        send(tile(a, t, g), tile(a, t, g), agy_s.at[phase, t], agy_r.at[phase, t], yl_peer)
+        send(tile(phase, a, t, g), tile(phase, a, t, g), agy_s.at[phase, t], agy_r.at[phase, t], yl_peer)
 
     def gather_spread(phase, a, t, who, slot):
         for d, h in ((0, 0), (1, 1), (0, 1), (1, 0)):
-            piece = half(a, t, who, h)
+            piece = half(phase, a, t, who, h)
             send(piece, piece, agz_s.at[phase, t, slot, d * 2 + h], agz_r.at[phase, t, who, d * 2 + h], z_peers[d])
 
     def gather_second(phase, a, t):
-        arrived(tile(a, t, other), agy_s.at[phase, t], agy_r.at[phase, t])
+        arrived(tile(phase, a, t, other), agy_s.at[phase, t], agy_r.at[phase, t])
         gather_spread(phase, a, t, other, 1)
 
     def gather_relay(phase, a, t, same):
         y = yl if same else 1 - yl
         for d, h, to in ((3, 0, 0), (1, 1, 1)):
             who = ((z + d) % 4) * 2 + y
-            piece = half(a, t, who, h)
+            piece = half(phase, a, t, who, h)
             arrived(piece, agz_s.at[phase, t, 0, 0], agz_r.at[phase, t, who, to * 3])
             send(piece, piece, agz_s.at[phase, t, 2, to * 2 + int(same)], agz_r.at[phase, t, who, to * 3], z_peers[to])
 
@@ -137,7 +141,7 @@
         for y in range(2):
             for d, h, k in ((3, 1, 1), (1, 0, 2), (2, 0, 0), (2, 1, 3)):
                 who = ((z + d) % 4) * 2 + y
-                arrived(half(a, t, who, h), agz_s.at[phase, t, 0, 0], agz_r.at[phase, t, who, k])
+                arrived(half(phase, a, t, who, h), agz_s.at[phase, t, 0, 0], agz_r.at[phase, t, who, k])
 
     far_row = (1 - yh) * 2 + co
 
@@ -161,11 +165,11 @@
         slab = dst.at[pl.ds(2 * row, 2)]
         send(slab, slab, wf_s.at[phase, 0], wf_r.at[phase, 0], sibling)
 
-    def weight_far(phase, dst):
-        for k, xs in enumerate([x] + x_at):
-            piece = weight_piece(dst, far_row, xs)
-            arrived(piece, w_s.at[phase, 0], w_r.at[phase, 1, xs])
-            send(piece, piece, wf_s.at[phase, 1 + k], wf_r.at[phase, 1 + k], sibling)
+    def weight_far(phase, dst, k):
+        xs = ([x] + x_at)[k]
+        piece = weight_piece(dst, far_row, xs)
+        arrived(piece, w_s.at[phase, 0], w_r.at[phase, 1, xs])
+        send(piece, piece, wf_s.at[phase, 1 + k], wf_r.at[phase, 1 + k], sibling)
 
     def weight_wait(phase, dst):
         arrived(dst.at[pl.ds(2 * (row + 1 - 2 * co), 2)], wf_s.at[phase, 0], wf_r.at[phase, 0])
@@ -190,34 +194,27 @@
         arrived(kv_slab(row + 1 - 2 * co), kvw_s.at[1], kvw_r.at[1])
         arrived(kv_slab(far_row + 1 - 2 * co), kvw_s.at[2], kvw_r.at[2])
 
-    def partial_one(a, weights, t, xd):
+    def partial_one(a, weights, first, size, xd):
         return jnp.dot(
-            a[pl.ds(t * B, B), :], weights[:, :, block(xd)].reshape(8 * B, B), preferred_element_type=F32
+            a[pl.ds(first, size), :], weights[:, :, block(xd)].reshape(8 * B, B), preferred_element_type=F32
         )
 
-    def partial_copy(phase, stage, got, t, k):
-        rows = pl.ds(t * B, B)
-        send(stage.at[k, rows], got.at[x, rows], rs_s.at[phase, t, k], rs_r.at[phase, t, x], x_peers[k])
-
-    def partial_make(phase, a, weights, stage, got, own, t):
-        rows = pl.ds(t * B, B)
+    def partial_make(a, weights, stage, own, first, size):
+        rows = pl.ds(first, size)
         for k, xd in enumerate(x_at):
-            stage[k, rows, :] = partial_one(a, weights, t, xd).astype(BF16)
-        own[rows, :] = partial_one(a, weights, t, x)
-
-    def partial_start(phase, stage, got, t):
-        for k in range(3):
-            partial_copy(phase, stage, got, t, k)
-
-    def partial_send(phase, a, weights, stage, got, own, t):
-        partial_make(phase, a, weights, stage, got, own, t)
-        partial_start(phase, stage, got, t)
-
-    def partial_sum(phase, got, own, t):
-        rows = pl.ds(t * B, B)
+            stage[k, rows, :] = partial_one(a, weights, first, size, xd).astype(BF16)
+        own[rows, :] = partial_one(a, weights, first, size, x)
+
+    def partial_start(phase, stage, got, u):
+        rows = pl.ds(u * HB, HB)
+        for k in (2, 0, 1):
+            send(stage.at[k, rows], got.at[x, rows], rs_s.at[phase, u, k], rs_r.at[phase, u, x], x_peers[k])
+
+    def partial_sum(phase, got, own, u):
+        rows = pl.ds(u * HB, HB)
         total = own[rows, :]
         for xs in x_at:
-            arrived(got.at[xs, rows], rs_s.at[phase, t, 0], rs_r.at[phase, t, xs])
+            arrived(got.at[xs, rows], rs_s.at[phase, u, 0], rs_r.at[phase, u, xs])
             total = total + got[xs, rows, :].astype(F32)
         return total
 
@@ -375,6 +372,8 @@
     gather_wait(0, a1, 2)
     kv_part(2)
     kv_reduce(1)
+    for k in range(3):
+        weight_far(0, w, k)
     gather_wait(0, a1, 3)
     kv_part(3)
     kv_reduce(2)
@@ -382,45 +381,50 @@
     for t in range(3):
         kv_relay(t)
 
-    weight_far(0, w)
-    weight_wait(0, w)
-    partial_make(0, a1, w, stage1, got1, own1, 0)
-    kv_relay(3)
-    partial_start(0, stage1, got1, 0)
     weight_down(1, wo, wout)
     weight_relay(1, wout, 0)
-    for t in range(1, CHUNKS):
-        partial_make(0, a1, w, stage1, got1, own1, t)
+    weight_relay(1, wout, 1)
+    weight_far(0, w, 3)
+    weight_wait(0, w)
+    partial_make(a1, w, stage1, own1, 0, B)
+    partial_start(0, stage1, got1, 0)
+    kv_relay(3)
+    partial_make(a1, w, stage1, own1, B, B)
     kv_own_wait()
-
-    for t in range(CHUNKS):
-        rows = pl.ds(t * B, B)
-        total = partial_sum(0, got1, own1, t)
-        scale = inv[rows, :] * SCALE
-        for h in range(2):
-            part = total[:, h * HEAD_DIM : (h + 1) * HEAD_DIM] * scale
-            part = part * cos[rows, :] + pltpu.roll(part, HEAD_DIM // 2, 1) * sin[rows, :]
-            q[pl.ds(h * B, B), :] = part.astype(BF16)
-        width = (t + 1) * B
+    partial_start(0, stage1, got1, 1)
+    partial_make(a1, w, stage1, own1, 2 * B, B)
+    partial_make(a1, w, stage1, own1, 3 * B, B)
+    partial_start(0, stage1, got1, 2)
+
+    def query_ready(u, n):
+        for v in range(n):
+            rows = pl.ds((u + v) * HB, HB)
+            total = partial_sum(0, got1, own1, u + v)
+            scale = inv[rows, :] * SCALE
+            for h in range(2):
+                part = total[:, h * HEAD_DIM : (h + 1) * HEAD_DIM] * scale
+                part = part * cos[rows, :] + pltpu.roll(part, HEAD_DIM // 2, 1) * sin[rows, :]
+                q[pl.ds((h * n + v) * HB, HB), :] = part.astype(BF16)
+
+    def attend(u, n):
+        count = n * HB
+        width = (u + n) * HB
+        queries = pl.ds(0, 2 * count)
         here = kvo[pl.ds(pl.multiple_of(row * TOK, TOK), width), :]
-        queries = q[...]
-        s = lax.dot_general(queries, here[:, :HEAD_DIM], along, preferred_element_type=F32)
-        query_at = lax.broadcasted_iota(jnp.int32, s.shape, 0) % B + t * B
+        s = lax.dot_general(q[queries, :], here[:, :HEAD_DIM], along, preferred_element_type=F32)
+        query_at = lax.broadcasted_iota(jnp.int32, s.shape, 0) % count + u * HB
         key_at = lax.broadcasted_iota(jnp.int32, s.shape, 1)
         s = jnp.where(key_at <= query_at, s, -1e30)
         top = jnp.max(s, axis=1, keepdims=True)
         p = jnp.exp2(s - top).astype(BF16)
         acc = jnp.dot(p, here[:, HEAD_DIM:], preferred_element_type=F32)
-
-        if t == 0:
+        if u == 0:
             kv_rest_wait()
-            for v in range(1, CHUNKS):
-                partial_start(0, stage1, got1, v)
 
         def step(kb, carry):
             top, acc = carry
             there = kvo[block(kb, TOK), :]
-            s = lax.dot_general(q[...], there[:, :HEAD_DIM], along, preferred_element_type=F32)
+            s = lax.dot_general(q[queries, :], there[:, :HEAD_DIM], along, preferred_element_type=F32)
             new = jnp.maximum(top, jnp.max(s, axis=1, keepdims=True))
             p = jnp.exp2(s - new).astype(BF16)
             acc = acc * jnp.exp2(top - new) + jnp.dot(p, there[:, HEAD_DIM:], preferred_element_type=F32)
@@ -428,38 +432,88 @@
 
         top, acc = lax.fori_loop(0, row, step, (top, acc))
         mixed = (acc[:, :HEAD_DIM] / acc[:, HEAD_DIM:]).astype(BF16)
-        a2[rows, block(g)] = jnp.concatenate([mixed[:B], mixed[B:]], axis=1)
-        gather_first(1, a2, t)
-        gather_spread(1, a2, t, g, 0)
-        if t == 0:
-            weight_relay(1, wout, 1)
-        if t == 1:
-            weight_relay(1, wout, 2)
-            weight_near(1, wout)
-        if t == 2:
-            gather_relay(1, a2, 0, False)
-        if t >= 1:
-            gather_second(1, a2, t - 1)
-            gather_relay(1, a2, t - 1, True)
-
+        a2[pl.ds(u * HB, count), block(g)] = jnp.concatenate([mixed[:count], mixed[count:]], axis=1)
+
+    def out_part(u):
+        gather_wait(1, a2, u)
+        partial_make(a2, wout, stage2, own2, u * HB, HB)
+        partial_start(1, stage2, got2, u)
+
+    def out_sum(u):
+        out[pl.ds(u * HB, HB), :] = partial_sum(1, got2, own2, u).astype(BF16)
+
+    def turn_out(u):
+        gather_first(1, a2, u)
+        gather_spread(1, a2, u, g, 0)
+
+    def turn_second(u):
+        gather_second(1, a2, u)
+        gather_relay(1, a2, u, True)
+
+    query_ready(0, 1)
+    attend(0, 1)
+    turn_out(0)
+    partial_start(0, stage1, got1, 3)
+    weight_relay(1, wout, 2)
+    weight_near(1, wout)
+
+    query_ready(1, 1)
+    attend(1, 1)
+    turn_out(1)
+    partial_start(0, stage1, got1, 4)
+    partial_start(0, stage1, got1, 5)
+
+    query_ready(2, 2)
+    attend(2, 2)
+    turn_out(2)
+    turn_out(3)
+    partial_start(0, stage1, got1, 6)
+    partial_start(0, stage1, got1, 7)
+    turn_second(0)
+    turn_second(1)
+    weight_far(1, wout, 0)
+    weight_far(1, wout, 1)
+    weight_far(1, wout, 2)
+
+    query_ready(4, 2)
+    attend(4, 2)
+    turn_out(4)
+    turn_out(5)
+    gather_relay(1, a2, 0, False)
     gather_relay(1, a2, 1, False)
-    weight_far(1, wout)
+    turn_second(2)
+    turn_second(3)
+    weight_far(1, wout, 3)
+
+    query_ready(6, 2)
+    attend(6, 2)
+    turn_out(6)
+    turn_out(7)
     weight_wait(1, wout)
-    gather_wait(1, a2, 0)
-    partial_send(1, a2, wout, stage2, got2, own2, 0)
-    gather_second(1, a2, 3)
     gather_relay(1, a2, 2, False)
-    gather_relay(1, a2, 3, True)
-    gather_wait(1, a2, 1)
-    partial_send(1, a2, wout, stage2, got2, own2, 1)
+    out_part(0)
     gather_relay(1, a2, 3, False)
-    gather_wait(1, a2, 2)
-    partial_send(1, a2, wout, stage2, got2, own2, 2)
-    out[pl.ds(0, B), :] = partial_sum(1, got2, own2, 0).astype(BF16)
-    gather_wait(1, a2, 3)
-    partial_send(1, a2, wout, stage2, got2, own2, 3)
-    for t in range(1, CHUNKS):
-        out[pl.ds(t * B, B), :] = partial_sum(1, got2, own2, t).astype(BF16)
+    turn_second(4)
+    out_part(1)
+    turn_second(5)
+    out_part(2)
+    turn_second(6)
+    gather_relay(1, a2, 4, False)
+    out_part(3)
+    turn_second(7)
+    gather_relay(1, a2, 5, False)
+    out_sum(0)
+    out_part(4)
+    gather_relay(1, a2, 6, False)
+    out_sum(1)
+    out_part(5)
+    gather_relay(1, a2, 7, False)
+    out_sum(2)
+    out_part(6)
+    out_sum(3)
+    out_part(7)
+    for u in range(4, TURNS):
+        out_sum(u)
 
     for copy in sent:
         copy.wait_send()
@@ -510,14 +564,14 @@
             pltpu.VMEM((TOK, 128), F32),
             pltpu.VMEM((TOK, HEAD_DIM), F32),
             pltpu.VMEM((TOK, HEAD_DIM), F32),
-            pltpu.VMEM((2 * B, HEAD_DIM), BF16),
+            pltpu.VMEM((4 * HB, HEAD_DIM), BF16),
             pltpu.VMEM((8, 1, TOK), F32),
             pltpu.VMEM((4, 1, TOK), F32),
             dma((6,)),
-            dma((2, CHUNKS)),
-            dma((2, CHUNKS)),
-            dma((2, CHUNKS, 3, 4)),
-            dma((2, CHUNKS, 8, 4)),
+            dma((2, TURNS)),
+            dma((2, TURNS)),
+            dma((2, TURNS, 3, 4)),
+            dma((2, TURNS, 8, 4)),
             dma((8,)),
             dma((8,)),
             dma((4,)),
@@ -528,8 +582,8 @@
             dma((2, 5)),
             dma((3,)),
             dma((3,)),
-            dma((2, CHUNKS, 4)),
-            dma((2, CHUNKS, 4)),
+            dma((2, TURNS, 4)),
+            dma((2, TURNS, 4)),
             dma((CHUNKS, 4)),
             dma((CHUNKS, 4)),
             dma((CHUNKS, 8)),
@@ -542,7 +596,7 @@
         ),
     )(
         activations,
-        norm_gain.reshape(1, B),
+        norm_gain,
         w_query.reshape(2, 4, B, B),
         w_key.reshape(2, 4, B, 1024),
         w_value.reshape(2, 4, B, 1024),

time: 133 us -> 130 us (0.977)
  no operation moved by 1% of the time
where the time goes in v4:
time: 130 us; the launch traced here: 129 us
  Pallas kernels  127 us (98%)
  local copies, waits for them, and re-layouts  1.87 us (1%)
    pallas_call x1, Pallas kernels, local_step(): pl.pallas_call(kernel, out_shape=jax.ShapeDtypeStruct((TOK, B), BF16), in...  127 us

profile of v4, /device:TPU:18, one launch (start us, length us, event | category | flops | bytes accessed | tf_op | source)
XLA Modules:
  0.0 129.1 jit_solution(12765627878259770617)
XLA Ops:
  0.0 127.2 %shard_map.82 = bf16[1024,256]{1,0:T(8,128)(2,1)} custom-call(bf16[1024,256]{1,0:T(8,128)(2,1)} %act.1, bf16[256]{0:T(256)(128)(2,1)} %gain.1, bf16[2,4,256,256]{3,2,1,0:T(8,128)(2,1)} %bitcast.6, bf16[2,4,256,1024]{3,2,1,0:T(8,128)(2,1)} %bitcast.4, bf16[2,4,256,1024]{3,2,1,0:T(8,128)(2,1)} %bitcast.5, bf16[2,4,256,256]{3,2,1,0:T(8,128)(2,1)} %bitcast.7, ...), custom_call_target="tpu_custom_call" | custom-call | tf_op jit(solution)/shard_map/pallas_call | solution.py:543
  127.2 1.9 %copy.10 = bf16[1024,256]{1,0:T(8,128)(2,1)} copy(bf16[1024,256]{1,0:T(8,128)(2,1)} %shard_map.82) | data formatting | bytes 1048576

commit v5 on v4

--- a/solution.py
+++ b/solution.py
@@ -113,17 +113,13 @@
         size = HB if phase else B
         return a.at[pl.ds(t * size, size), block(who)]
 
-    def half(phase, a, t, who, h):
-        size = HB // 2 if phase else B // 2
-        return a.at[pl.ds((2 * t + h) * size, size), block(who)]
-
     def gather_first(phase, a, t):
         send(tile(phase, a, t, g), tile(phase, a, t, g), agy_s.at[phase, t], agy_r.at[phase, t], yl_peer)
 
     def gather_spread(phase, a, t, who, slot):
-        for d, h in ((0, 0), (1, 1), (0, 1), (1, 0)):
-            piece = half(phase, a, t, who, h)
-            send(piece, piece, agz_s.at[phase, t, slot, d * 2 + h], agz_r.at[phase, t, who, d * 2 + h], z_peers[d])
+        piece = tile(phase, a, t, who)
+        for d in (0, 1) if t % 2 == 0 else (1, 0):
+            send(piece, piece, agz_s.at[phase, t, slot, d], agz_r.at[phase, t, who, d], z_peers[d])
 
     def gather_second(phase, a, t):
         arrived(tile(phase, a, t, other), agy_s.at[phase, t], agy_r.at[phase, t])
@@ -131,17 +127,18 @@
 
     def gather_relay(phase, a, t, same):
         y = yl if same else 1 - yl
-        for d, h, to in ((3, 0, 0), (1, 1, 1)):
-            who = ((z + d) % 4) * 2 + y
-            piece = half(phase, a, t, who, h)
-            arrived(piece, agz_s.at[phase, t, 0, 0], agz_r.at[phase, t, who, to * 3])
-            send(piece, piece, agz_s.at[phase, t, 2, to * 2 + int(same)], agz_r.at[phase, t, who, to * 3], z_peers[to])
+        to = t % 2
+        who = ((z + (3, 1)[to]) % 4) * 2 + y
+        piece = tile(phase, a, t, who)
+        arrived(piece, agz_s.at[phase, t, 0, 0], agz_r.at[phase, t, who, to])
+        send(piece, piece, agz_s.at[phase, t, 2, int(same)], agz_r.at[phase, t, who, to], z_peers[to])
 
     def gather_wait(phase, a, t):
+        to = t % 2
         for y in range(2):
-            for d, h, k in ((3, 1, 1), (1, 0, 2), (2, 0, 0), (2, 1, 3)):
+            for d, k in (((1, 1), (2, 0)) if to == 0 else ((3, 0), (2, 1))):
                 who = ((z + d) % 4) * 2 + y
-                arrived(half(phase, a, t, who, h), agz_s.at[phase, t, 0, 0], agz_r.at[phase, t, who, k])
+                arrived(tile(phase, a, t, who), agz_s.at[phase, t, 0, 0], agz_r.at[phase, t, who, k])
 
     far_row = (1 - yh) * 2 + co
 
@@ -489,25 +486,25 @@
     attend(6, 2)
     turn_out(6)
     turn_out(7)
+    turn_second(4)
     weight_wait(1, wout)
     gather_relay(1, a2, 2, False)
     out_part(0)
     gather_relay(1, a2, 3, False)
-    turn_second(4)
+    turn_second(5)
     out_part(1)
-    turn_second(5)
+    gather_relay(1, a2, 4, False)
+    turn_second(6)
     out_part(2)
-    turn_second(6)
-    gather_relay(1, a2, 4, False)
+    gather_relay(1, a2, 5, False)
+    turn_second(7)
     out_part(3)
-    turn_second(7)
-    gather_relay(1, a2, 5, False)
     out_sum(0)
+    gather_relay(1, a2, 6, False)
     out_part(4)
-    gather_relay(1, a2, 6, False)
     out_sum(1)
+    gather_relay(1, a2, 7, False)
     out_part(5)
-    gather_relay(1, a2, 7, False)
     out_sum(2)
     out_part(6)
     out_sum(3)
@@ -570,8 +567,8 @@
             dma((6,)),
             dma((2, TURNS)),
             dma((2, TURNS)),
-            dma((2, TURNS, 3, 4)),
-            dma((2, TURNS, 8, 4)),
+            dma((2, TURNS, 3, 2)),
+            dma((2, TURNS, 8, 2)),
             dma((8,)),
             dma((8,)),
             dma((4,)),

time: 130 us -> 127 us (0.977)
  Pallas kernels: 127 us -> 124 us
    pallas_call x1, Pallas kernels: 127 us -> 124 us  [local_step(): pl.pallas_call(kernel, out_shape=jax.ShapeDtypeStruct((TOK, B), BF16), in...]
where the time goes in v5:
time: 127 us; the launch traced here: 126 us
  Pallas kernels  124 us (98%)
  local copies, waits for them, and re-layouts  1.87 us (1%)
    pallas_call x1, Pallas kernels, local_step(): pl.pallas_call(kernel, out_shape=jax.ShapeDtypeStruct((TOK, B), BF16), in...  124 us

profile of v5, /device:TPU:18, one launch (start us, length us, event | category | flops | bytes accessed | tf_op | source)
XLA Modules:
  0.0 125.6 jit_solution(11458975081501631380)
XLA Ops:
  0.0 123.7 %shard_map.82 = bf16[1024,256]{1,0:T(8,128)(2,1)} custom-call(bf16[1024,256]{1,0:T(8,128)(2,1)} %act.1, bf16[256]{0:T(256)(128)(2,1)} %gain.1, bf16[2,4,256,256]{3,2,1,0:T(8,128)(2,1)} %bitcast.6, bf16[2,4,256,1024]{3,2,1,0:T(8,128)(2,1)} %bitcast.4, bf16[2,4,256,1024]{3,2,1,0:T(8,128)(2,1)} %bitcast.5, bf16[2,4,256,256]{3,2,1,0:T(8,128)(2,1)} %bitcast.7, ...), custom_call_target="tpu_custom_call" | custom-call | tf_op jit(solution)/shard_map/pallas_call | solution.py:540
  123.7 1.9 %copy.10 = bf16[1024,256]{1,0:T(8,128)(2,1)} copy(bf16[1024,256]{1,0:T(8,128)(2,1)} %shard_map.82) | data formatting | bytes 1048576
